TPU v7x, 32 devices: a whole 2x2x4 slice. The times are simulated.
32 devices in a mesh: tm: 8 (over z, x), chan: 4 (over y, core).
Axes of the slice: x: 2, y: 2, z: 4, core: 2. Of those that a mesh axis runs over, the one named last changes fastest.
Arguments:
- visibilities: bfloat16 [8, 8, 128, 512], P('tm', None, None, 'chan'), may hold values from -6 to 6
- station_gains: float32 [8, 192, 512], P(None, 'chan'), may hold values from -1.5 to 1.5, as said below
- station_pairs: int32 [128, 2], replicated, may hold values from 0 to 191, as said below
- average_bands: int32 [128, 2], replicated, may hold values from 0 to 3, as said below
- tile_map: int32 [128, 8], replicated, may hold values from 0 to 63
- baseline_order: int32 [128], replicated, may hold values from 0 to 127, as said below
Outputs:
- averaged: bfloat16 [8, 8, 128, 512], P(None, None, 'tm', 'chan')
- gridded: float32 [64, 8, 512], P('tm', None, 'chan')
Inputs may be any that keep to these rules, and one draw needn't show every extreme that they name: `station_pairs`: row b holds the two stations of baseline b, the first smaller than the second. `average_bands`: column 0 is at most 3, column 1 at most 2. In each aligned block of 16 positions k of baseline_order, the bands of the baselines baseline_order[k] are, in some order, the pairs (3 - j % (3 + 1), 2 - j % (2 + 1)) for j = 0 to 15. `baseline_order`: each baseline once. `station_gains`: diagonal Jones entries have magnitudes of order one.
All inputs are finite; a program needn't handle non-finite values.
Results may differ from a plain program's by a relative error of at most 0.019.
Values may be sent and summed in bfloat16 or wider, within the bound.
A program may use at most 128 MiB of HBM per device.

v0:
```python
import jax
import jax.numpy as jnp
from jax import lax
from jax.sharding import PartitionSpec as P

TILE_DEV = 8
TLOG = 3
CLOG = 2


def product(left, right):
    return (left[0] * right[0] - left[1] * right[1], left[0] * right[1] + left[1] * right[0])


def product_conj(left, right):
    return (left[0] * right[0] + left[1] * right[1], left[1] * right[0] - left[0] * right[1])


def add_pair(left, right):
    return (left[0] + right[0], left[1] + right[1])


def as_matrix(components):
    return [
        [(components[0], components[1]), (components[2], components[3])],
        [(components[4], components[5]), (components[6], components[7])],
    ]


def jones_apply(first, middle, second):
    left_gain = as_matrix(first)
    coherency = as_matrix(middle)
    right_gain = as_matrix(second)
    partial_rows = [
        [
            add_pair(
                product(left_gain[i][0], coherency[0][k]), product(left_gain[i][1], coherency[1][k])
            )
            for k in range(2)
        ]
        for i in range(2)
    ]
    result = []
    for i in range(2):
        for c in range(2):
            element = add_pair(
                product_conj(partial_rows[i][0], right_gain[c][0]),
                product_conj(partial_rows[i][1], right_gain[c][1]),
            )
            result.extend(element)
    return result


def calibrate(samples, gain_table, first_station, second_station):
    left_gain = jnp.take(gain_table, first_station, axis=1)
    right_gain = jnp.take(gain_table, second_station, axis=1)
    values = [samples[:, i].astype(jnp.float32) for i in range(8)]
    result = jones_apply(
        [left_gain[i][None] for i in range(8)], values, [right_gain[i][None] for i in range(8)]
    )
    return jnp.stack(result, axis=1).astype(jnp.bfloat16)


def halve_time(current, size):
    extent = current.shape[0]
    shaped = current.reshape((extent // size, 2, size // 2) + current.shape[1:])
    merged = 0.5 * (shaped[:, 0:1] + shaped[:, 1:2])
    return jnp.broadcast_to(merged, shaped.shape).reshape(current.shape)


def halve_chan(current, size):
    extent = current.shape[-1]
    shaped = current.reshape(current.shape[:-1] + (extent // size, 2, size // 2))
    merged = 0.5 * (shaped[..., 0:1, :] + shaped[..., 1:2, :])
    return jnp.broadcast_to(merged, shaped.shape).reshape(current.shape)


def band_average(samples, time_levels, chan_levels):
    values = samples.astype(jnp.float32)
    time_select = time_levels[None, None, :, None]
    chan_select = chan_levels[None, None, :, None]
    result = values
    current = values
    for k in range(1, TLOG + 1):
        current = halve_time(current, 2**k)
        result = jnp.where(time_select >= k, current, result)
    final = result
    current = result
    for k in range(1, CLOG + 1):
        current = halve_chan(current, 2**k)
        final = jnp.where(chan_select >= k, current, final)
    return final.astype(jnp.bfloat16)


def shards(visibilities, station_gains, station_pairs, average_bands, tile_map, baseline_order):
    chan_width = visibilities.shape[3]
    block_size = visibilities.shape[2] // lax.axis_size("tm")
    all_gains = lax.all_gather(station_gains, "chan", axis=1, tiled=True)
    gain_table = lax.dynamic_slice_in_dim(
        all_gains, lax.axis_index("chan") * chan_width, chan_width, 2
    )
    reordered = jnp.take(visibilities, baseline_order, axis=2)
    rows_here = lax.dynamic_slice_in_dim(
        baseline_order, lax.axis_index("tm") * block_size, block_size
    )
    bands_here = average_bands[rows_here]
    ordered_pairs = station_pairs[baseline_order]
    payload = calibrate(reordered, gain_table, ordered_pairs[:, 0], ordered_pairs[:, 1])
    turned = lax.all_to_all(payload, "tm", split_axis=2, concat_axis=0, tiled=True)
    averaged = band_average(turned, bands_here[:, 0], bands_here[:, 1])
    tile_here = tile_map[rows_here].T
    time_index = jnp.arange(averaged.shape[0], dtype=jnp.int32)[:, None]
    period = jnp.left_shift(jnp.ones_like(bands_here[:, 0]), bands_here[:, 0])[None, :]
    tile_ids = jnp.where(time_index % period == 0, tile_here, -1)
    targets = jnp.arange(TILE_DEV * lax.axis_size("tm"), dtype=jnp.int32)
    one_hot = (tile_ids[None] == targets[:, None, None]).astype(jnp.bfloat16)
    gridded = lax.psum_scatter(
        jnp.einsum("rtb,tkbc->rkc", one_hot, averaged, preferred_element_type=jnp.float32).astype(
            jnp.bfloat16
        ),
        "tm",
        scatter_dimension=0,
        tiled=True,
    ).astype(jnp.float32)
    return (averaged, gridded)


def solution(mesh):
    return jax.shard_map(
        shards,
        mesh=mesh,
        in_specs=(P("tm", None, None, "chan"), P(None, "chan", None), P(), P(), P(), P()),
        out_specs=(P(None, None, "tm", "chan"), P("tm", None, "chan")),
        check_vma=False,
    )
```

profile of v0, /device:TPU:0, one launch (start us, length us, event | category | flops | bytes accessed | tf_op | source)
XLA Modules:
  0.0 150.5 jit_solution(9269000064630720570)
XLA Ops:
  7.2 0.0 all-gather.2.cloned.1.call-start
  7.3 2.5 %copy.535 = f32[8,48,512]{2,0,1:T(8,128)} copy(f32[8,48,512]{2,1,0:T(8,128)} %param.9) | data formatting | bytes 1572864 | tf_op args[1]
  9.8 0.0 all-gather.2.cloned.1.call-update
  9.8 0.0 copy-done.7
  9.8 0.1 copy.534
  9.9 0.1 copy.533
  10.1 0.1 copy.554
  10.2 0.1 compare_select_fusion.4
  10.2 0.6 gather_fusion
  10.8 0.6 gather_fusion.3
  11.4 0.2 copy.575
  11.6 0.6 gather_fusion.1
  12.2 0.7 gather_fusion.2
  12.9 0.2 slice_reduce_fusion
  13.1 0.1 shift-left_reduce_fusion
  13.3 0.1 bitcast_select_fusion.1
  13.4 27.8 %all-gather.2.cloned.1.call-done = f32[8,192,512]{2,0,1:T(8,128)} async-done(((f32[8,48,512]{2,0,1:T(8,128)}), f32[8,192,512]{2,0,1:T(8,128)}) %all-gather.2.cloned.1.call-update) | async-done | bytes 3145744 | tf_op jit(solution)/shard_map/all_gather | solution.py:98
  41.2 1.2 constant_dynamic-slice_fusion
  42.4 0.8 gather_fusion.5
  43.1 0.8 gather_fusion.4
  43.9 0.2 fusion.12
  44.1 0.2 fusion.13
  44.3 0.1 bitcast_dynamic-update-slice_fusion.7
  44.5 0.1 bitcast_dynamic-update-slice_fusion.3
  44.8 0.9 copy.540
  45.7 5.5 %all-to-all-start = ((bf16[1,8,128,128]{3,1,0,2:T(8,128)(2,1)}), bf16[1,8,128,128]{3,1,0,2:T(8,128)(2,1)S(1)}, u32[]{:S(2)}, u32[]{:S(2)}) async-start(bf16[1,8,128,128]{3,1,0,2:T(8,128)(2,1)} %copy.540), calls=%async_computation | async-start | bytes 524288 | tf_op jit(solution)/shard_map/all_to_all | solution.py:109
  51.2 0.0 reduce-scatter.4.cloned.1.call-start
  51.2 0.2 bitcast_select_fusion.2
  51.4 0.1 copy.555
  51.5 0.2 compare_reduce_fusion.4
  51.7 8.8 %all-to-all-done = bf16[1,8,128,128]{3,1,0,2:T(8,128)(2,1)S(1)} async-done(((bf16[1,8,128,128]{3,1,0,2:T(8,128)(2,1)}), bf16[1,8,128,128]{3,1,0,2:T(8,128)(2,1)S(1)}, u32[]{:S(2)}, u32[]{:S(2)}) %all-to-all-start) | async-done | bytes 262176 | tf_op jit(solution)/shard_map/all_to_all | solution.py:109
  60.5 0.8 convert_bitcast_fusion
  61.4 0.7 fusion.58
  62.2 0.7 copy.542
  62.9 0.1 fusion.59
  63.0 0.1 fusion.5
  63.1 0.9 fusion.6
  64.0 0.8 fusion.56
  64.8 1.6 %copy.543 = f32[4,8,16,128]{2,1,3,0:T(8,128)S(1)} copy(f32[4,8,16,128]{3,2,0,1:T(8,128)} %fusion.58) | data formatting | bytes 524288 | tf_op jit(solution)/shard_map/broadcast_in_dim | solution.py:68
  66.5 0.3 copy.563
  66.8 3.5 %copy.544 = f32[8,1,8,16,128]{3,2,4,0,1:T(8,128)} copy(f32[8,1,8,16,128]{4,3,0,2,1:T(8,128)} %convert_bitcast_fusion) | data formatting | bytes 1048576 | tf_op jit(solution)/shard_map/convert_element_type | solution.py:79
  70.3 0.3 broadcast_in_dim.121
  70.6 0.3 broadcast_in_dim.118
  70.8 1.9 %copy-done = f32[8,1,8,16,128]{3,2,4,0,1:T(8,128)S(1)} copy-done((f32[8,1,8,16,128]{3,2,4,0,1:T(8,128)S(1)}, f32[8,1,8,16,128]{3,2,4,0,1:T(8,128)}, u32[]{:S(2)}) %copy-start) | copy-done | bytes 524312
  72.7 0.1 copy-done.4
  72.8 0.8 select_select_fusion
  73.7 1.6 %fusion.57 = f32[8,8,16,64]{2,1,3,0:T(8,128)} fusion(f32[8,8,16,64,2,1]{2,1,4,3,0,5:T(8,128)S(1)} %select_select_fusion), kind=kLoop, calls=%fused_computation.150 | loop fusion | flops 131072 | bytes 786432 | tf_op jit(solution)/shard_map/broadcast_in_dim | solution.py:75
  75.3 0.2 fusion
  75.5 0.8 copy-done.3
  76.3 0.2 copy.549
  76.5 0.1 fusion.4
  76.6 1.5 copy-done.1
  78.1 0.3 broadcast_in_dim.127
  78.3 1.4 copy.552
  79.8 0.3 broadcast_in_dim.124
  80.1 1.4 copy.553
  81.6 0.3 fusion.11
  81.9 0.3 fusion.2
  82.2 0.7 copy.576
  82.9 0.0 reduce-scatter.4.cloned.1.call-update
  82.9 0.7 copy.556
  83.6 58.7 %reduce-scatter.4.cloned.1.call-done = bf16[8,1024]{1,0:T(8,128)(2,1)} async-done(((bf16[64,1024]{1,0:T(8,128)(2,1)}), bf16[8,1024]{1,0:T(8,128)(2,1)}) %reduce-scatter.4.cloned.1.call-update) | async-done | bytes 16400
  142.3 0.7 bitcast_convert_fusion
  143.1 0.6 copy.557
  (36 shorter events, 0.5 us)
Async XLA Ops:
  7.2 2.6 %copy-start.7 = (s32[128,2]{0,1:T(2,128)S(1)}, s32[128,2]{0,1:T(2,128)}, u32[]{:S(2)}) copy-start(s32[128,2]{0,1:T(2,128)} %param.10) | copy-start | bytes 3076
  7.2 2.8 %copy-start.8 = (s32[128,2]{0,1:T(2,128)S(1)}, s32[128,2]{0,1:T(2,128)}, u32[]{:S(2)}) copy-start(s32[128,2]{0,1:T(2,128)} %param.11) | copy-start | bytes 3076
  7.2 2.9 %copy-start.6 = (s32[128,8]{0,1:T(8,128)S(1)}, s32[128,8]{0,1:T(8,128)}, u32[]{:S(2)}) copy-start(s32[128,8]{0,1:T(8,128)} %param.12) | copy-start | bytes 12292
  7.2 3.0 %copy-start.9 = (s32[128]{0:T(128)S(1)}, s32[128]{0:T(128)}, u32[]{:S(2)}) copy-start(s32[128]{0:T(128)} %param.13) | copy-start | bytes 1540
  7.2 4.2 %copy-start.5 = (bf16[1,8,128,128]{3,2,1,0:T(8,128)(2,1)S(1)}, bf16[1,8,128,128]{3,2,1,0:T(8,128)(2,1)}, u32[]{:S(2)}) copy-start(bf16[1,8,128,128]{3,2,1,0:T(8,128)(2,1)} %param.8) | copy-start | bytes 786436
  7.2 34.0 %all-gather.2.cloned.1.call-start = ((), (), s32[]{:S(2)}) async-start(), calls=%async_computation.2 | async-start | bytes 3932160 | tf_op jit(solution)/shard_map/all_gather | solution.py:98
  45.7 14.8 %all-to-all-start = ((bf16[1,8,128,128]{3,1,0,2:T(8,128)(2,1)}), bf16[1,8,128,128]{3,1,0,2:T(8,128)(2,1)S(1)}, u32[]{:S(2)}, u32[]{:S(2)}) async-start(bf16[1,8,128,128]{3,1,0,2:T(8,128)(2,1)} %copy.540), calls=%async_computation | async-start | bytes 524288 | tf_op jit(solution)/shard_map/all_to_all | solution.py:109
  51.2 91.2 %reduce-scatter.4.cloned.1.call-start = ((), (), s32[]{:S(2)}) async-start(), calls=%async_computation.3 | async-start | bytes 147456
  70.5 2.2 %copy-start = (f32[8,1,8,16,128]{3,2,4,0,1:T(8,128)S(1)}, f32[8,1,8,16,128]{3,2,4,0,1:T(8,128)}, u32[]{:S(2)}) copy-start(f32[8,1,8,16,128]{3,2,4,0,1:T(8,128)} %copy.544) | copy-start | bytes 1572868
  70.6 2.3 %copy-start.4 = (f32[1,1,8,16,128]{3,2,4,1,0:T(8,128)S(1)}, f32[1,1,8,16,128]{3,2,4,1,0:T(8,128)}, u32[]{:S(2)}) copy-start(f32[1,1,8,16,128]{3,2,4,1,0:T(8,128)} %fusion.6) | copy-start | bytes 196612
  75.3 1.0 copy-start.3
  76.5 1.6 %copy-start.1 = (f32[8,8,16,64]{2,1,3,0:T(8,128)S(1)}, f32[8,8,16,64]{2,1,3,0:T(8,128)}, u32[]{:S(2)}) copy-start(f32[8,8,16,64]{2,1,3,0:T(8,128)} %fusion.57) | copy-start | bytes 786436
  79.8 1.7 %copy-start.2 = (f32[4,8,16,128]{3,2,0,1:T(8,128)S(1)}, f32[4,8,16,128]{3,2,0,1:T(8,128)}, u32[]{:S(2)}) copy-start(f32[4,8,16,128]{3,2,0,1:T(8,128)} %fusion.58) | copy-start | bytes 786436
Sparse Core Ops, SparseCore 0:
  9.9 31.2 all-gather.1
  83.0 59.2 reduce-scatter.3
where the time goes:
time: 151 us
  waiting for transfers between devices  95.3 us (63%)
  local copies, waits for them, and re-layouts  26 us (17%)
  between operations  14.4 us (10%)
  other arithmetic  8.95 us (6%)
  starting transfers between devices  5.59 us (4%)
    unnamed x3, waiting for transfers between devices  58.8 us
    all_gather x1, waiting for transfers between devices, shards(): all_gains = lax.all_gather(station_gains, 'chan', axis=1, tiled=True)  27.8 us
    unnamed x29, local copies, waits for them, and re-layouts  9.66 us
    all_to_all x1, waiting for transfers between devices, shards(): lax.all_to_all(payload, 'tm', split_axis=2, concat_axis=0, tiled=True)  8.78 us
    all_to_all x1, starting transfers between devices, shards(): lax.all_to_all(payload, 'tm', split_axis=2, concat_axis=0, tiled=True)  5.51 us
    convert_element_type x1, local copies, waits for them, and re-layouts, band_average(): values = samples.astype(jnp.float32)  3.49 us
  transfers between devices with their start and end apart: 3, of which 3 were waited for; matrix products, arithmetic and copies ran while one was open for 3% of the time, Pallas kernels for 0%

commit v1 on v0

v1 whole, which is shorter than its diff:
```python
import functools

import jax
import jax.numpy as jnp
from jax import lax
from jax.experimental import pallas as pl
from jax.experimental.pallas import tpu as pltpu
from jax.sharding import PartitionSpec as P

TLOG = 3
CLOG = 2
LANES = 128
MESH = pl.DeviceIdType.MESH
F32 = jnp.float32
BF16 = jnp.bfloat16

ORDER, FIRST, SECOND, TBAND, CBAND, TILE0 = range(6)


def product(left, right):
    return (left[0] * right[0] - left[1] * right[1], left[0] * right[1] + left[1] * right[0])


def product_conj(left, right):
    return (left[0] * right[0] + left[1] * right[1], left[1] * right[0] - left[0] * right[1])


def add_pair(left, right):
    return (left[0] + right[0], left[1] + right[1])


def as_matrix(components):
    return [
        [(components[0], components[1]), (components[2], components[3])],
        [(components[4], components[5]), (components[6], components[7])],
    ]


def jones_apply(first, middle, second):
    left_gain = as_matrix(first)
    coherency = as_matrix(middle)
    right_gain = as_matrix(second)
    partial_rows = [
        [
            add_pair(
                product(left_gain[i][0], coherency[0][k]), product(left_gain[i][1], coherency[1][k])
            )
            for k in range(2)
        ]
        for i in range(2)
    ]
    result = []
    for i in range(2):
        for c in range(2):
            element = add_pair(
                product_conj(partial_rows[i][0], right_gain[c][0]),
                product_conj(partial_rows[i][1], right_gain[c][1]),
            )
            result.extend(element)
    return result


def split(values, width):
    return [values[:, i * width : (i + 1) * width] for i in range(8)]


def iota(shape, axis):
    return lax.broadcasted_iota(jnp.int32, shape, axis)


def dot(left, right):
    return jnp.dot(left, right, preferred_element_type=F32)


def one_hot(column, ids):
    return jnp.where(column == ids, 1.0, 0.0).astype(BF16)


def channel_means(width):
    row = iota((width, width), 0)
    column = iota((width, width), 1)
    means = []
    for level in range(1, CLOG + 1):
        same = (row >> level) == (column >> level)
        means.append(jnp.where(same, 2.0**-level, 0.0))
    return jnp.concatenate(means, axis=1).astype(BF16)


def channel_average(samples, means, level, width):
    averaged = dot(samples, means)
    result = samples.astype(F32)
    for k in range(1, CLOG + 1):
        result = jnp.where(level >= k, averaged[:, (k - 1) * width : k * width], result)
    return result


def kernel(
    n_tm, n_chan, vis_ref, gain_ref, index_ref, avg_ref, grid_ref,
    send, turned, gain_send, gains, table, chosen, calibrated, tiles_send, tiles,
    turn_out, turn_in, gain_out, gain_in, tile_out, tile_in,
):
    me = lax.axis_index("tm")
    mine = lax.axis_index("chan")
    baselines = vis_ref.shape[2]
    width = vis_ref.shape[3]
    rows = baselines // n_tm
    stations = gain_ref.shape[1]
    padded = gain_send.shape[1]
    tile_rows = grid_ref.shape[0]
    n_tiles = tile_rows * n_tm

    barrier = pltpu.get_barrier_semaphore()
    for step in range(1, n_tm):
        pl.semaphore_signal(
            barrier, inc=1, device_id={"tm": lax.rem(me + step, n_tm)}, device_id_type=MESH
        )
    for step in range(1, n_chan):
        pl.semaphore_signal(
            barrier, inc=1, device_id={"chan": lax.rem(mine + step, n_chan)}, device_id_type=MESH
        )

    index = index_ref[...]
    place = one_hot(index[:, ORDER : ORDER + 1], iota((baselines, baselines), 1))
    raw = jnp.concatenate([vis_ref[0, i] for i in range(8)], axis=1)
    send[...] = dot(place, raw).astype(BF16).reshape(send.shape)
    for c in range(n_chan):
        block = jnp.concatenate(
            [gain_ref[i, :, c * width : (c + 1) * width] for i in range(8)], axis=1
        )
        if padded > stations:
            block = jnp.concatenate(
                [block, jnp.zeros((padded - stations, 8 * width), F32)], axis=0
            )
        gain_send[c] = block.astype(BF16)

    pl.semaphore_wait(barrier, n_tm + n_chan - 2)

    copies = []
    gain_copies = []
    for step in range(1, n_chan):
        other = lax.rem(mine + step, n_chan)
        copy = pltpu.make_async_remote_copy(
            src_ref=gain_send.at[other],
            dst_ref=gains.at[mine],
            send_sem=gain_out.at[other],
            recv_sem=gain_in.at[mine],
            device_id={"chan": other},
            device_id_type=MESH,
        )
        copy.start()
        copies.append(copy)
    for step in range(1, n_tm):
        other = lax.rem(me + step, n_tm)
        copy = pltpu.make_async_remote_copy(
            src_ref=send.at[other],
            dst_ref=turned.at[me],
            send_sem=turn_out.at[other],
            recv_sem=turn_in.at[me],
            device_id={"tm": other},
            device_id_type=MESH,
        )
        copy.start()
        copies.append(copy)

    turned[me] = send[me]
    gains[mine] = gain_send[mine]
    means = channel_means(width)
    table[...] = dot(place, index.astype(F32).astype(BF16))

    ids = iota((1, n_chan * padded), 1)
    if padded > stations:
        lane = ids
        for c in range(n_chan):
            inside = (lane >= c * padded) & (lane < c * padded + stations)
            ids = jnp.where(inside, lane - c * (padded - stations), ids)
            ids = jnp.where((lane >= c * padded + stations) & (lane < (c + 1) * padded), -1, ids)
    here = pl.ds(pl.multiple_of(me * rows, rows), rows)
    at_all = table[...].astype(jnp.int32)
    at_here = table[here, :].astype(jnp.int32)
    pick = jnp.concatenate(
        [
            one_hot(at_all[:, FIRST : FIRST + 1], ids),
            one_hot(at_all[:, SECOND : SECOND + 1], ids),
            one_hot(at_here[:, FIRST : FIRST + 1], ids),
            one_hot(at_here[:, SECOND : SECOND + 1], ids),
        ],
        axis=0,
    )
    period = jnp.left_shift(jnp.ones((baselines, 1), jnp.int32), at_all[:, TBAND : TBAND + 1])
    start = me - (me & (period - 1))
    lane = iota((baselines, LANES), 1)
    tile = jnp.sum(
        jnp.where(lane == start + TILE0, table[...], 0.0), axis=1, keepdims=True
    ).astype(jnp.int32)
    wide = max(n_tiles, LANES)
    share = jnp.where(
        tile == iota((baselines, wide), 1), 1.0 / period.astype(F32), 0.0
    )
    share = share.T[:n_tiles].astype(BF16)

    for step in range(1, n_chan):
        other = lax.rem(mine + step, n_chan)
        pltpu.make_async_remote_copy(
            src_ref=gain_send.at[other],
            dst_ref=gains.at[other],
            send_sem=gain_out.at[other],
            recv_sem=gain_in.at[other],
            device_id={"chan": other},
            device_id_type=MESH,
        ).wait_recv()
    chosen[...] = dot(pick, gains[...].reshape(n_chan * padded, 8 * width))

    def calibrate_block(k, carry):
        at = pl.ds(pl.multiple_of(k * rows, rows), rows)
        at_second = pl.ds(pl.multiple_of(baselines + k * rows, rows), rows)
        result = jones_apply(
            split(chosen[at, :], width),
            split(send[k].astype(F32), width),
            split(chosen[at_second, :], width),
        )
        calibrated[at, :] = jnp.concatenate(result, axis=1).astype(BF16)
        return carry

    lax.fori_loop(0, n_tm, calibrate_block, 0, unroll=2)
    level = at_all[:, CBAND : CBAND + 1]
    sums = []
    for i in range(8):
        part = channel_average(calibrated[:, i * width : (i + 1) * width], means, level, width)
        sums.append(dot(share, part.astype(BF16)).reshape(n_tm, tile_rows, width))
    tiles_send[...] = jnp.concatenate(sums, axis=1).astype(BF16)
    for step in range(1, n_tm):
        other = lax.rem(me + step, n_tm)
        copy = pltpu.make_async_remote_copy(
            src_ref=tiles_send.at[other],
            dst_ref=tiles.at[me],
            send_sem=tile_out.at[other],
            recv_sem=tile_in.at[me],
            device_id={"tm": other},
            device_id_type=MESH,
        )
        copy.start()
        copies.append(copy)
    tiles[me] = tiles_send[me]

    for step in range(1, n_tm):
        other = lax.rem(me + step, n_tm)
        pltpu.make_async_remote_copy(
            src_ref=send.at[other],
            dst_ref=turned.at[other],
            send_sem=turn_out.at[other],
            recv_sem=turn_in.at[other],
            device_id={"tm": other},
            device_id_type=MESH,
        ).wait_recv()
    left = split(chosen[2 * baselines : 2 * baselines + rows, :], width)
    right = split(chosen[2 * baselines + rows : 2 * baselines + 2 * rows, :], width)

    def calibrate_time(t, carry):
        result = jones_apply(left, split(turned[t].astype(F32), width), right)
        at = pl.ds(pl.multiple_of(t * rows, rows), rows)
        calibrated[at, :] = jnp.concatenate(result, axis=1).astype(BF16)
        return carry

    lax.fori_loop(0, n_tm, calibrate_time, 0, unroll=2)
    group = 2**TLOG
    time_level = jnp.broadcast_to(at_here[:, TBAND : TBAND + 1], (rows, width))
    chan_level = jnp.broadcast_to(at_here[:, CBAND : CBAND + 1], (rows, width))
    chan_level = jnp.concatenate([chan_level] * group, axis=0)
    for first in range(0, n_tm, group):
        at = slice(first * rows, (first + group) * rows)
        for i in range(8):
            part = channel_average(
                calibrated[at, i * width : (i + 1) * width], means, chan_level, width
            )
            current = [part[t * rows : (t + 1) * rows] for t in range(group)]
            result = list(current)
            for k in range(1, TLOG + 1):
                current = [
                    0.5 * (current[2 * j] + current[2 * j + 1]) for j in range(len(current) // 2)
                ]
                result = [
                    jnp.where(time_level >= k, current[t >> k], result[t]) for t in range(group)
                ]
            for t in range(group):
                avg_ref[first + t, i] = result[t].astype(BF16)

    for step in range(1, n_tm):
        other = lax.rem(me + step, n_tm)
        pltpu.make_async_remote_copy(
            src_ref=tiles_send.at[other],
            dst_ref=tiles.at[other],
            send_sem=tile_out.at[other],
            recv_sem=tile_in.at[other],
            device_id={"tm": other},
            device_id_type=MESH,
        ).wait_recv()
    total = tiles[0].astype(F32)
    for m in range(1, n_tm):
        total = total + tiles[m].astype(F32)
    for i in range(8):
        grid_ref[:, i, :] = total[i * tile_rows : (i + 1) * tile_rows]
    for copy in copies:
        copy.wait_send()


def shards(n_tm, n_chan, tile_count, visibilities, station_gains, station_pairs, average_bands, tile_map, baseline_order):
    baselines, width = visibilities.shape[2:]
    rows = baselines // n_tm
    stations = station_gains.shape[1]
    padded = -(-stations // 16) * 16
    tile_rows = tile_count // n_tm
    index = jnp.concatenate(
        [baseline_order[:, None], station_pairs, average_bands, tile_map], axis=1
    )
    index = jnp.pad(index, ((0, 0), (0, LANES - index.shape[1])))
    vmem = pl.BlockSpec(memory_space=pltpu.VMEM)
    dma = pltpu.SemaphoreType.DMA
    return pl.pallas_call(
        functools.partial(kernel, n_tm, n_chan),
        out_shape=(
            jax.ShapeDtypeStruct((n_tm, 8, rows, width), BF16),
            jax.ShapeDtypeStruct((tile_rows, 8, width), F32),
        ),
        in_specs=[vmem] * 3,
        out_specs=(vmem, vmem),
        scratch_shapes=[
            pltpu.VMEM((n_tm, rows, 8 * width), BF16),
            pltpu.VMEM((n_tm, rows, 8 * width), BF16),
            pltpu.VMEM((n_chan, padded, 8 * width), BF16),
            pltpu.VMEM((n_chan, padded, 8 * width), BF16),
            pltpu.VMEM((baselines, LANES), F32),
            pltpu.VMEM((2 * baselines + 2 * rows, 8 * width), F32),
            pltpu.VMEM((baselines, 8 * width), BF16),
            pltpu.VMEM((n_tm, 8 * tile_rows, width), BF16),
            pltpu.VMEM((n_tm, 8 * tile_rows, width), BF16),
            dma((n_tm,)),
            dma((n_tm,)),
            dma((n_chan,)),
            dma((n_chan,)),
            dma((n_tm,)),
            dma((n_tm,)),
        ],
        compiler_params=pltpu.CompilerParams(
            collective_id=0, has_side_effects=True, vmem_limit_bytes=40 * 2**20
        ),
        cost_estimate=pl.CostEstimate(
            flops=2 * 10**8, bytes_accessed=2 * 10**6, transcendentals=0
        ),
    )(visibilities, station_gains, index)


def solution(mesh):
    n_tm, n_chan = mesh.shape["tm"], mesh.shape["chan"]
    tile_count = 8 * n_tm
    return jax.shard_map(
        functools.partial(shards, n_tm, n_chan, tile_count),
        mesh=mesh,
        in_specs=(P("tm", None, None, "chan"), P(None, "chan", None), P(), P(), P(), P()),
        out_specs=(P(None, None, "tm", "chan"), P("tm", None, "chan")),
        check_vma=False,
    )
```

time: 151 us -> 22.7 us (0.15)
  waiting for transfers between devices: 95.3 us -> 0 us
  local copies, waits for them, and re-layouts: 26 us -> 4.2 us
  Pallas kernels: 0 us -> 16.9 us
  between operations: 14.4 us -> 0.67 us
  other arithmetic: 8.95 us -> 0.71 us
  starting transfers between devices: 5.59 us -> 0 us
    unnamed x3 -> x0, waiting for transfers between devices: 58.8 us -> none
    all_gather x1 -> x0, waiting for transfers between devices: 27.8 us -> none  [shards(): all_gains = lax.all_gather(station_gains, 'chan', axis=1, tiled=True)]
    pallas_call x0 -> x1, Pallas kernels: none -> 16.9 us  [shards(): pl.pallas_call(functools.partial(kernel, n_tm, n_chan), out_shape=(jax.Sh...]
    all_to_all x1 -> x0, waiting for transfers between devices: 8.78 us -> none  [shards(): lax.all_to_all(payload, 'tm', split_axis=2, concat_axis=0, tiled=True)]
    unnamed x29 -> x10, local copies, waits for them, and re-layouts: 9.66 us -> 4.08 us
    all_to_all x1 -> x0, starting transfers between devices: 5.51 us -> none  [shards(): lax.all_to_all(payload, 'tm', split_axis=2, concat_axis=0, tiled=True)]
    broadcast_in_dim x8 -> x0, local copies, waits for them, and re-layouts: 4.23 us -> none  [the longest x5 2.25 us: halve_time(): return jnp.broadcast_to(merged, shaped.shape).reshape(current.shape)]
    gather x6 -> x0, local copies, waits for them, and re-layouts: 3.98 us -> none  [the longest x1 0.76 us: calibrate(): right_gain = jnp.take(gain_table, second_station, axis=1)]
  transfers between devices with their start and end apart: 3 -> 0, of which waited for: 3 -> 0; matrix products, arithmetic and copies ran while one was open for 3% -> 0% of each run, Pallas kernels for 0% -> 0%
where the time goes in v1:
time: 22.7 us; the launch traced here: 22.5 us
  Pallas kernels  16.9 us (74%)
  local copies, waits for them, and re-layouts  4.2 us (19%)
  other arithmetic  0.71 us (3%)
  between operations  0.67 us (3%)
    pallas_call x1, Pallas kernels, shards(): pl.pallas_call(functools.partial(kernel, n_tm, n_chan), out_shape=(jax.Sh...  16.9 us
    unnamed x10, local copies, waits for them, and re-layouts  4.08 us
    concatenate x1, other arithmetic, shards(): jnp.concatenate([baseline_order[:, None], station_pairs, average_bands, t...  0.71 us

profile of v1, /device:TPU:0, one launch (start us, length us, event | category | flops | bytes accessed | tf_op | source)
XLA Modules:
  0.0 22.5 jit_solution(16274165424825912583)
XLA Ops:
  0.6 0.0 copy-start.3
  0.6 0.0 copy-start.2
  0.7 0.6 %copy-done.3 = s32[128]{0:T(128)S(1)} copy-done((s32[128]{0:T(128)S(1)}, s32[128]{0:T(128)}, u32[]{:S(2)}) %copy-start.3) | copy-done | bytes 536
  1.3 0.0 copy-done.2
  1.3 0.7 %pad_add_fusion = s32[128,13]{0,1:T(8,128)S(1)} fusion(s32[128,8]{0,1:T(8,128)} %param.10, s32[128,2]{0,1:T(2,128)S(1)} %copy-done.2, s32[128,2]{0,1:T(2,128)} %param.8, s32[128,1]{0,1:T(1,128)S(1)} %bitcast.1), kind=kLoop, calls=%fused_computation | loop fusion | flops 4992 | bytes 13312 | tf_op jit(solution)/shard_map/concatenate | solution.py:312
  2.0 0.1 copy.12
  2.2 0.0 copy-start
  2.2 1.1 %copy-done = f32[8,48,512]{2,1,0:T(8,128)S(1)} copy-done((f32[8,48,512]{2,1,0:T(8,128)S(1)}, f32[8,48,512]{2,1,0:T(8,128)}, u32[]{:S(2)}) %copy-start) | copy-done | bytes 786456
  3.3 0.0 copy-start.1
  3.3 0.9 %copy-done.1 = bf16[1,8,128,128]{3,2,1,0:T(8,128)(2,1)S(1)} copy-done((bf16[1,8,128,128]{3,2,1,0:T(8,128)(2,1)S(1)}, bf16[1,8,128,128]{3,2,1,0:T(8,128)(2,1)}, u32[]{:S(2)}) %copy-start.1) | copy-done | bytes 262168
  4.2 16.9 %shard_map.77 = (bf16[8,8,16,128]{3,2,1,0:T(8,128)(2,1)S(1)}, f32[8,8,128]{2,1,0:T(8,128)S(1)}) custom-call(bf16[1,8,128,128]{3,2,1,0:T(8,128)(2,1)S(1)} %copy-done.1, f32[8,48,512]{2,1,0:T(8,128)S(1)} %copy-done, s32[128,128]{1,0:T(8,128)S(1)} %pad.4.index_ref), custom_call_target="tpu_custom_call" | custom-call | flops 200000000 | bytes 2000000 | tf_op jit(solution)/shard_map/pallas_call | solution.py:318
  21.2 0.7 %copy.15 = bf16[8,8,16,128]{3,2,1,0:T(8,128)(2,1)} copy(bf16[8,8,16,128]{3,2,1,0:T(8,128)(2,1)S(1)} %get-tuple-element.4) | data formatting | bytes 524288
  21.9 0.6 %copy.16 = f32[8,8,128]{2,1,0:T(8,128)} copy(f32[8,8,128]{2,1,0:T(8,128)S(1)} %get-tuple-element.5) | data formatting | bytes 65536
  (1 shorter events, 0.0 us)
Async XLA Ops:
  0.6 0.7 %copy-start.3 = (s32[128]{0:T(128)S(1)}, s32[128]{0:T(128)}, u32[]{:S(2)}) copy-start(s32[128]{0:T(128)} %param.11) | copy-start | bytes 1540
  0.6 0.7 %copy-start.2 = (s32[128,2]{0,1:T(2,128)S(1)}, s32[128,2]{0,1:T(2,128)}, u32[]{:S(2)}) copy-start(s32[128,2]{0,1:T(2,128)} %param.9) | copy-start | bytes 3076
  2.2 1.1 %copy-start = (f32[8,48,512]{2,1,0:T(8,128)S(1)}, f32[8,48,512]{2,1,0:T(8,128)}, u32[]{:S(2)}) copy-start(f32[8,48,512]{2,1,0:T(8,128)} %gain_ref.1) | copy-start | bytes 2359300
  3.3 0.9 %copy-start.1 = (bf16[1,8,128,128]{3,2,1,0:T(8,128)(2,1)S(1)}, bf16[1,8,128,128]{3,2,1,0:T(8,128)(2,1)}, u32[]{:S(2)}) copy-start(bf16[1,8,128,128]{3,2,1,0:T(8,128)(2,1)} %vis_ref.1) | copy-start | bytes 786436

commit v2 on v1

--- a/solution.py
+++ b/solution.py
@@ -13,8 +13,6 @@
 MESH = pl.DeviceIdType.MESH
 F32 = jnp.float32
 BF16 = jnp.bfloat16
-
-ORDER, FIRST, SECOND, TBAND, CBAND, TILE0 = range(6)
 
 
 def product(left, right):
@@ -95,19 +93,32 @@
 
 
 def kernel(
-    n_tm, n_chan, vis_ref, gain_ref, index_ref, avg_ref, grid_ref,
+    n_tm, n_chan,
+    vis_hbm, gain_hbm, pairs_hbm, bands_hbm, map_hbm, order_hbm, avg_ref, grid_ref,
+    vis_ref, gain_ref, pairs_ref, bands_ref, map_ref, order_ref, local, index,
     send, turned, gain_send, gains, table, chosen, calibrated, tiles_send, tiles,
     turn_out, turn_in, gain_out, gain_in, tile_out, tile_in,
 ):
     me = lax.axis_index("tm")
     mine = lax.axis_index("chan")
-    baselines = vis_ref.shape[2]
-    width = vis_ref.shape[3]
+    baselines = vis_ref.shape[1]
+    width = vis_ref.shape[2]
     rows = baselines // n_tm
     stations = gain_ref.shape[1]
     padded = gain_send.shape[1]
     tile_rows = grid_ref.shape[0]
     n_tiles = tile_rows * n_tm
+    times = map_ref.shape[0]
+    first_at, second_at, time_at, chan_at = range(times, times + 4)
+
+    sources = (order_hbm, gain_hbm, vis_hbm.at[0], pairs_hbm, bands_hbm, map_hbm)
+    targets = (order_ref, gain_ref, vis_ref, pairs_ref, bands_ref, map_ref)
+    loads = [
+        pltpu.make_async_copy(source, target, local.at[i])
+        for i, (source, target) in enumerate(zip(sources, targets))
+    ]
+    for load in loads:
+        load.start()
 
     barrier = pltpu.get_barrier_semaphore()
     for step in range(1, n_tm):
@@ -119,10 +130,10 @@
             barrier, inc=1, device_id={"chan": lax.rem(mine + step, n_chan)}, device_id_type=MESH
         )
 
-    index = index_ref[...]
-    place = one_hot(index[:, ORDER : ORDER + 1], iota((baselines, baselines), 1))
-    raw = jnp.concatenate([vis_ref[0, i] for i in range(8)], axis=1)
-    send[...] = dot(place, raw).astype(BF16).reshape(send.shape)
+    index[...] = jnp.zeros_like(index)
+    loads[0].wait()
+    place = jnp.where(order_ref[...] == iota((baselines, baselines), 0), 1.0, 0.0)
+    loads[1].wait()
     for c in range(n_chan):
         block = jnp.concatenate(
             [gain_ref[i, :, c * width : (c + 1) * width] for i in range(8)], axis=1
@@ -132,6 +143,11 @@
                 [block, jnp.zeros((padded - stations, 8 * width), F32)], axis=0
             )
         gain_send[c] = block.astype(BF16)
+
+    place = place.T.astype(BF16)
+    loads[2].wait()
+    raw = jnp.concatenate([vis_ref[i] for i in range(8)], axis=1)
+    send[...] = dot(place, raw).astype(BF16).reshape(send.shape)
 
     pl.semaphore_wait(barrier, n_tm + n_chan - 2)
 
@@ -165,7 +181,14 @@
     turned[me] = send[me]
     gains[mine] = gain_send[mine]
     means = channel_means(width)
-    table[...] = dot(place, index.astype(F32).astype(BF16))
+    for load in loads[3:]:
+        load.wait()
+    index[:times] = map_ref[...].astype(F32)
+    index[first_at : second_at + 1] = pairs_ref[...].astype(F32)
+    index[time_at : chan_at + 1] = bands_ref[...].astype(F32)
+    table[...] = lax.dot_general(
+        place, index[...].astype(BF16), (((1,), (1,)), ((), ())), preferred_element_type=F32
+    )
 
     ids = iota((1, n_chan * padded), 1)
     if padded > stations:
@@ -179,18 +202,18 @@
     at_here = table[here, :].astype(jnp.int32)
     pick = jnp.concatenate(
         [
-            one_hot(at_all[:, FIRST : FIRST + 1], ids),
-            one_hot(at_all[:, SECOND : SECOND + 1], ids),
-            one_hot(at_here[:, FIRST : FIRST + 1], ids),
-            one_hot(at_here[:, SECOND : SECOND + 1], ids),
+            one_hot(at_all[:, first_at : first_at + 1], ids),
+            one_hot(at_all[:, second_at : second_at + 1], ids),
+            one_hot(at_here[:, first_at : first_at + 1], ids),
+            one_hot(at_here[:, second_at : second_at + 1], ids),
         ],
         axis=0,
     )
-    period = jnp.left_shift(jnp.ones((baselines, 1), jnp.int32), at_all[:, TBAND : TBAND + 1])
+    period = jnp.left_shift(jnp.ones((baselines, 1), jnp.int32), at_all[:, time_at : time_at + 1])
     start = me - (me & (period - 1))
     lane = iota((baselines, LANES), 1)
     tile = jnp.sum(
-        jnp.where(lane == start + TILE0, table[...], 0.0), axis=1, keepdims=True
+        jnp.where(lane == start, table[...], 0.0), axis=1, keepdims=True
     ).astype(jnp.int32)
     wide = max(n_tiles, LANES)
     share = jnp.where(
@@ -222,7 +245,7 @@
         return carry
 
     lax.fori_loop(0, n_tm, calibrate_block, 0, unroll=2)
-    level = at_all[:, CBAND : CBAND + 1]
+    level = at_all[:, chan_at : chan_at + 1]
     sums = []
     for i in range(8):
         part = channel_average(calibrated[:, i * width : (i + 1) * width], means, level, width)
@@ -263,8 +286,8 @@
 
     lax.fori_loop(0, n_tm, calibrate_time, 0, unroll=2)
     group = 2**TLOG
-    time_level = jnp.broadcast_to(at_here[:, TBAND : TBAND + 1], (rows, width))
-    chan_level = jnp.broadcast_to(at_here[:, CBAND : CBAND + 1], (rows, width))
+    time_level = jnp.broadcast_to(at_here[:, time_at : time_at + 1], (rows, width))
+    chan_level = jnp.broadcast_to(at_here[:, chan_at : chan_at + 1], (rows, width))
     chan_level = jnp.concatenate([chan_level] * group, axis=0)
     for first in range(0, n_tm, group):
         at = slice(first * rows, (first + group) * rows)
@@ -309,21 +332,26 @@
     stations = station_gains.shape[1]
     padded = -(-stations // 16) * 16
     tile_rows = tile_count // n_tm
-    index = jnp.concatenate(
-        [baseline_order[:, None], station_pairs, average_bands, tile_map], axis=1
-    )
-    index = jnp.pad(index, ((0, 0), (0, LANES - index.shape[1])))
     vmem = pl.BlockSpec(memory_space=pltpu.VMEM)
     dma = pltpu.SemaphoreType.DMA
+    hbm = functools.partial(pltpu.with_memory_space_constraint, memory_space=pltpu.HBM)
     return pl.pallas_call(
         functools.partial(kernel, n_tm, n_chan),
         out_shape=(
-            jax.ShapeDtypeStruct((n_tm, 8, rows, width), BF16),
-            jax.ShapeDtypeStruct((tile_rows, 8, width), F32),
+            pltpu.VMEM((n_tm, 8, rows, width), BF16),
+            pltpu.VMEM((tile_rows, 8, width), F32),
         ),
-        in_specs=[vmem] * 3,
+        in_specs=[pl.BlockSpec(memory_space=pl.ANY)] * 6,
         out_specs=(vmem, vmem),
         scratch_shapes=[
+            pltpu.VMEM((8, baselines, width), BF16),
+            pltpu.VMEM(station_gains.shape, F32),
+            pltpu.VMEM((2, baselines), jnp.int32),
+            pltpu.VMEM((2, baselines), jnp.int32),
+            pltpu.VMEM((n_tm, baselines), jnp.int32),
+            pltpu.VMEM((1, baselines), jnp.int32),
+            dma((6,)),
+            pltpu.VMEM((LANES, baselines), F32),
             pltpu.VMEM((n_tm, rows, 8 * width), BF16),
             pltpu.VMEM((n_tm, rows, 8 * width), BF16),
             pltpu.VMEM((n_chan, padded, 8 * width), BF16),
@@ -346,7 +374,14 @@
         cost_estimate=pl.CostEstimate(
             flops=2 * 10**8, bytes_accessed=2 * 10**6, transcendentals=0
         ),
-    )(visibilities, station_gains, index)
+    )(
+        hbm(visibilities),
+        hbm(station_gains),
+        hbm(station_pairs.T),
+        hbm(average_bands.T),
+        hbm(tile_map.T),
+        hbm(baseline_order.reshape(1, baselines)),
+    )
 
 
 def solution(mesh):

time: 22.7 us -> 19.1 us (0.84)
  local copies, waits for them, and re-layouts: 4.2 us -> 1.32 us
  other arithmetic: 0.71 us -> 0 us
    unnamed x10 -> x2, local copies, waits for them, and re-layouts: 4.08 us -> 1.32 us
    concatenate x1 -> x0, other arithmetic: 0.71 us -> none  [shards(): jnp.concatenate([baseline_order[:, None], station_pairs, average_bands, t...]
where the time goes in v2:
time: 19.1 us; the launch traced here: 18.8 us
  Pallas kernels  16.8 us (88%)
  local copies, waits for them, and re-layouts  1.32 us (7%)
  between operations  0.64 us (3%)
    pallas_call x1, Pallas kernels, shards(): pl.pallas_call(functools.partial(kernel, n_tm, n_chan), out_shape=(pltpu....  16.8 us
    unnamed x2, local copies, waits for them, and re-layouts  1.32 us

profile of v2, /device:TPU:0, one launch (start us, length us, event | category | flops | bytes accessed | tf_op | source)
XLA Modules:
  0.0 18.8 jit_solution(12592970148140136404)
XLA Ops:
  0.6 16.8 %shard_map.77 = (bf16[8,8,16,128]{3,2,1,0:T(8,128)(2,1)S(1)}, f32[8,8,128]{2,1,0:T(8,128)S(1)}) custom-call(bf16[1,8,128,128]{3,2,1,0:T(8,128)(2,1)} %vis_hbm.1, f32[8,48,512]{2,1,0:T(8,128)} %gain_hbm.1, s32[2,128]{1,0:T(2,128)} %bitcast.5, s32[2,128]{1,0:T(2,128)} %bitcast.6, s32[8,128]{1,0:T(8,128)} %bitcast.4, s32[1,128]{1,0:T(1,128)} %bitcast.7), custom_call_target="tpu_custom_call" | custom-call | flops 200000000 | bytes 2000000 | tf_op jit(solution)/shard_map/pallas_call | solution.py:338
  17.4 0.7 %copy.10 = bf16[8,8,16,128]{3,2,1,0:T(8,128)(2,1)} copy(bf16[8,8,16,128]{3,2,1,0:T(8,128)(2,1)S(1)} %get-tuple-element.2) | data formatting | bytes 524288
  18.1 0.6 %copy.11 = f32[8,8,128]{2,1,0:T(8,128)} copy(f32[8,8,128]{2,1,0:T(8,128)S(1)} %get-tuple-element.3) | data formatting | bytes 65536

commit v3 on v2

--- a/solution.py
+++ b/solution.py
@@ -94,7 +94,7 @@
 
 def kernel(
     n_tm, n_chan,
-    vis_hbm, gain_hbm, pairs_hbm, bands_hbm, map_hbm, order_hbm, avg_ref, grid_ref,
+    vis_hbm, gain_hbm, pairs_hbm, bands_hbm, map_hbm, order_hbm, avg_ref, tiles_ref,
     vis_ref, gain_ref, pairs_ref, bands_ref, map_ref, order_ref, local, index,
     send, turned, gain_send, gains, table, chosen, calibrated, tiles_send, tiles,
     turn_out, turn_in, gain_out, gain_in, tile_out, tile_in,
@@ -106,7 +106,7 @@
     rows = baselines // n_tm
     stations = gain_ref.shape[1]
     padded = gain_send.shape[1]
-    tile_rows = grid_ref.shape[0]
+    tile_rows = tiles_ref.shape[1] // 8
     n_tiles = tile_rows * n_tm
     times = map_ref.shape[0]
     first_at, second_at, time_at, chan_at = range(times, times + 4)
@@ -317,13 +317,24 @@
             device_id={"tm": other},
             device_id_type=MESH,
         ).wait_recv()
-    total = tiles[0].astype(F32)
-    for m in range(1, n_tm):
-        total = total + tiles[m].astype(F32)
-    for i in range(8):
-        grid_ref[:, i, :] = total[i * tile_rows : (i + 1) * tile_rows]
+    tiles_ref[...] = tiles[...]
     for copy in copies:
         copy.wait_send()
+
+
+def write_kernel(avg_ref, tiles_ref, avg_hbm, grid_hbm, grid, done):
+    averaged = pltpu.make_async_copy(avg_ref, avg_hbm, done.at[0])
+    averaged.start()
+    tile_rows = grid.shape[0]
+    total = tiles_ref[0].astype(F32)
+    for m in range(1, tiles_ref.shape[0]):
+        total = total + tiles_ref[m].astype(F32)
+    for i in range(8):
+        grid[:, i, :] = total[i * tile_rows : (i + 1) * tile_rows]
+    gridded = pltpu.make_async_copy(grid, grid_hbm, done.at[1])
+    gridded.start()
+    averaged.wait()
+    gridded.wait()
 
 
 def shards(n_tm, n_chan, tile_count, visibilities, station_gains, station_pairs, average_bands, tile_map, baseline_order):
@@ -335,11 +346,11 @@
     vmem = pl.BlockSpec(memory_space=pltpu.VMEM)
     dma = pltpu.SemaphoreType.DMA
     hbm = functools.partial(pltpu.with_memory_space_constraint, memory_space=pltpu.HBM)
-    return pl.pallas_call(
+    averaged, tiles = pl.pallas_call(
         functools.partial(kernel, n_tm, n_chan),
         out_shape=(
             pltpu.VMEM((n_tm, 8, rows, width), BF16),
-            pltpu.VMEM((tile_rows, 8, width), F32),
+            pltpu.VMEM((n_tm, 8 * tile_rows, width), BF16),
         ),
         in_specs=[pl.BlockSpec(memory_space=pl.ANY)] * 6,
         out_specs=(vmem, vmem),
@@ -382,6 +393,17 @@
         hbm(tile_map.T),
         hbm(baseline_order.reshape(1, baselines)),
     )
+    return pl.pallas_call(
+        write_kernel,
+        out_shape=(
+            pltpu.HBM(averaged.shape, BF16),
+            pltpu.HBM((tile_rows, 8, width), F32),
+        ),
+        in_specs=[vmem] * 2,
+        out_specs=(pl.BlockSpec(memory_space=pltpu.HBM),) * 2,
+        scratch_shapes=[pltpu.VMEM((tile_rows, 8, width), F32), dma((2,))],
+        cost_estimate=pl.CostEstimate(flops=10**6, bytes_accessed=10**6, transcendentals=0),
+    )(averaged, tiles)
 
 
 def solution(mesh):

time: 19.1 us -> 20.8 us (1.089)
  Pallas kernels: 16.8 us -> 18.5 us
    pallas_call x0 -> x1, Pallas kernels: none -> 1.7 us  [shards(): pl.pallas_call(write_kernel, out_shape=(pltpu.HBM(averaged.shape, BF16),...]
    unnamed x2 -> x4, local copies, waits for them, and re-layouts: 1.32 us -> 1.35 us
where the time goes in v3:
time: 20.8 us; the launch traced here: 20.5 us
  Pallas kernels  18.5 us (89%)
  local copies, waits for them, and re-layouts  1.35 us (6%)
  between operations  0.65 us (3%)
    pallas_call x1, Pallas kernels, shards(): pl.pallas_call(functools.partial(kernel, n_tm, n_chan), out_shape=(pltpu....  16.8 us
    pallas_call x1, Pallas kernels, shards(): pl.pallas_call(write_kernel, out_shape=(pltpu.HBM(averaged.shape, BF16),...  1.7 us
    unnamed x4, local copies, waits for them, and re-layouts  1.35 us

profile of v3, /device:TPU:0, one launch (start us, length us, event | category | flops | bytes accessed | tf_op | source)
XLA Modules:
  0.0 20.5 jit_solution(14802699838565448554)
XLA Ops:
  0.6 16.8 %shard_map.77 = (bf16[8,8,16,128]{3,2,1,0:T(8,128)(2,1)S(1)}, bf16[8,64,128]{2,1,0:T(8,128)(2,1)S(1)}) custom-call(bf16[1,8,128,128]{3,2,1,0:T(8,128)(2,1)} %vis_hbm.1, f32[8,48,512]{2,1,0:T(8,128)} %gain_hbm.1, s32[2,128]{1,0:T(2,128)} %bitcast.5, s32[2,128]{1,0:T(2,128)} %bitcast.6, s32[8,128]{1,0:T(8,128)} %bitcast.4, s32[1,128]{1,0:T(1,128)} %bitcast.7), custom_call_target="tpu_custom_call" | custom-call | flops 200000000 | bytes 2000000 | tf_op jit(solution)/shard_map/pallas_call | solution.py:349
  17.4 0.0 copy-start
  17.4 0.7 %copy-done = bf16[8,8,16,128]{3,2,1,0:T(8,128)(2,1)} copy-done((bf16[8,8,16,128]{3,2,1,0:T(8,128)(2,1)}, bf16[8,8,16,128]{3,2,1,0:T(8,128)(2,1)S(1)}, u32[]{:S(2)}) %copy-start) | copy-done | bytes 262168
  18.1 0.0 copy-start.1
  18.1 0.7 %copy-done.1 = bf16[8,64,128]{2,1,0:T(8,128)(2,1)} copy-done((bf16[8,64,128]{2,1,0:T(8,128)(2,1)}, bf16[8,64,128]{2,1,0:T(8,128)(2,1)S(1)}, u32[]{:S(2)}) %copy-start.1) | copy-done | bytes 131096
  18.8 1.7 %shard_map.78 = (bf16[8,8,16,128]{3,2,1,0:T(8,128)(2,1)}, f32[8,8,128]{2,1,0:T(8,128)}) custom-call(bf16[8,8,16,128]{3,2,1,0:T(8,128)(2,1)} %copy-done, bf16[8,64,128]{2,1,0:T(8,128)(2,1)} %copy-done.1), custom_call_target="tpu_custom_call" | custom-call | flops 1000000 | bytes 1000000 | tf_op jit(solution)/shard_map/pallas_call | solution.py:396
Async XLA Ops:
  17.4 0.7 %copy-start = (bf16[8,8,16,128]{3,2,1,0:T(8,128)(2,1)}, bf16[8,8,16,128]{3,2,1,0:T(8,128)(2,1)S(1)}, u32[]{:S(2)}) copy-start(bf16[8,8,16,128]{3,2,1,0:T(8,128)(2,1)S(1)} %get-tuple-element.4.avg_ref) | copy-start | bytes 786436
  18.1 0.7 %copy-start.1 = (bf16[8,64,128]{2,1,0:T(8,128)(2,1)}, bf16[8,64,128]{2,1,0:T(8,128)(2,1)S(1)}, u32[]{:S(2)}) copy-start(bf16[8,64,128]{2,1,0:T(8,128)(2,1)S(1)} %get-tuple-element.5.tiles_ref) | copy-start | bytes 393220

commit v4 on v3

--- a/solution.py
+++ b/solution.py
@@ -346,6 +346,7 @@
     vmem = pl.BlockSpec(memory_space=pltpu.VMEM)
     dma = pltpu.SemaphoreType.DMA
     hbm = functools.partial(pltpu.with_memory_space_constraint, memory_space=pltpu.HBM)
+    near = functools.partial(pltpu.with_memory_space_constraint, memory_space=pltpu.VMEM)
     averaged, tiles = pl.pallas_call(
         functools.partial(kernel, n_tm, n_chan),
         out_shape=(
@@ -402,8 +403,9 @@
         in_specs=[vmem] * 2,
         out_specs=(pl.BlockSpec(memory_space=pltpu.HBM),) * 2,
         scratch_shapes=[pltpu.VMEM((tile_rows, 8, width), F32), dma((2,))],
+        compiler_params=pltpu.CompilerParams(vmem_limit_bytes=8 * 2**20),
         cost_estimate=pl.CostEstimate(flops=10**6, bytes_accessed=10**6, transcendentals=0),
-    )(averaged, tiles)
+    )(near(averaged), near(tiles))
 
 
 def solution(mesh):

time: 20.8 us -> 18.4 us (0.88)
  local copies, waits for them, and re-layouts: 1.35 us -> 0 us
  Pallas kernels: 18.5 us -> 17.5 us
    unnamed x4 -> x0, local copies, waits for them, and re-layouts: 1.35 us -> none
    pallas_call x1, Pallas kernels: 1.7 us -> 0.72 us  [shards(): pl.pallas_call(write_kernel, out_shape=(pltpu.HBM(averaged.shape, BF16),...]
where the time goes in v4:
time: 18.4 us; the launch traced here: 18.1 us
  Pallas kernels  17.5 us (95%)
  between operations  0.64 us (3%)
    pallas_call x1, Pallas kernels, shards(): pl.pallas_call(functools.partial(kernel, n_tm, n_chan), out_shape=(pltpu....  16.8 us
    pallas_call x1, Pallas kernels, shards(): pl.pallas_call(write_kernel, out_shape=(pltpu.HBM(averaged.shape, BF16),...  0.72 us

profile of v4, /device:TPU:0, one launch (start us, length us, event | category | flops | bytes accessed | tf_op | source)
XLA Modules:
  0.0 18.1 jit_solution(2849467093319907770)
XLA Ops:
  0.6 16.8 %shard_map.77 = (bf16[8,8,16,128]{3,2,1,0:T(8,128)(2,1)S(1)}, bf16[8,64,128]{2,1,0:T(8,128)(2,1)S(1)}) custom-call(bf16[1,8,128,128]{3,2,1,0:T(8,128)(2,1)} %vis_hbm.1, f32[8,48,512]{2,1,0:T(8,128)} %gain_hbm.1, s32[2,128]{1,0:T(2,128)} %bitcast.5, s32[2,128]{1,0:T(2,128)} %bitcast.6, s32[8,128]{1,0:T(8,128)} %bitcast.4, s32[1,128]{1,0:T(1,128)} %bitcast.7), custom_call_target="tpu_custom_call" | custom-call | flops 200000000 | bytes 2000000 | tf_op jit(solution)/shard_map/pallas_call | solution.py:350
  17.4 0.7 %shard_map.78 = (bf16[8,8,16,128]{3,2,1,0:T(8,128)(2,1)}, f32[8,8,128]{2,1,0:T(8,128)}) custom-call(bf16[8,8,16,128]{3,2,1,0:T(8,128)(2,1)S(1)} %get-tuple-element.4.avg_ref, bf16[8,64,128]{2,1,0:T(8,128)(2,1)S(1)} %get-tuple-element.5.tiles_ref), custom_call_target="tpu_custom_call" | custom-call | flops 1000000 | bytes 1000000 | tf_op jit(solution)/shard_map/pallas_call | solution.py:397

commit v5 on v4

v5 whole, which is shorter than its diff:
```python
import functools

import jax
import jax.numpy as jnp
from jax import lax
from jax.experimental import pallas as pl
from jax.experimental.pallas import tpu as pltpu
from jax.sharding import PartitionSpec as P

TLOG = 3
CLOG = 2
LANES = 128
MESH = pl.DeviceIdType.MESH
F32 = jnp.float32
BF16 = jnp.bfloat16


def product(left, right):
    return (left[0] * right[0] - left[1] * right[1], left[0] * right[1] + left[1] * right[0])


def product_conj(left, right):
    return (left[0] * right[0] + left[1] * right[1], left[1] * right[0] - left[0] * right[1])


def add_pair(left, right):
    return (left[0] + right[0], left[1] + right[1])


def as_matrix(components):
    return [
        [(components[0], components[1]), (components[2], components[3])],
        [(components[4], components[5]), (components[6], components[7])],
    ]


def jones_apply(first, middle, second):
    left_gain = as_matrix(first)
    coherency = as_matrix(middle)
    right_gain = as_matrix(second)
    partial_rows = [
        [
            add_pair(
                product(left_gain[i][0], coherency[0][k]), product(left_gain[i][1], coherency[1][k])
            )
            for k in range(2)
        ]
        for i in range(2)
    ]
    result = []
    for i in range(2):
        for c in range(2):
            element = add_pair(
                product_conj(partial_rows[i][0], right_gain[c][0]),
                product_conj(partial_rows[i][1], right_gain[c][1]),
            )
            result.extend(element)
    return result


def split(values, width):
    return [values[:, i * width : (i + 1) * width] for i in range(values.shape[1] // width)]


def iota(shape, axis):
    return lax.broadcasted_iota(jnp.int32, shape, axis)


def dot(left, right):
    return jnp.dot(left, right, preferred_element_type=F32)


def one_hot(column, ids):
    return jnp.where(column == ids, 1.0, 0.0).astype(BF16)


def channel_means(width):
    row = iota((width, width), 0)
    column = iota((width, width), 1)
    means = []
    for level in range(1, CLOG + 1):
        same = (row >> level) == (column >> level)
        means.append(jnp.where(same, 2.0**-level, 0.0))
    return jnp.concatenate(means, axis=1).astype(BF16)


def row_times(row, middle):
    return [
        add_pair(product(row[0], middle[0][b]), product(row[1], middle[1][b])) for b in range(2)
    ]


def times_row_conj(partial, row):
    return add_pair(product_conj(partial[0], row[0]), product_conj(partial[1], row[1]))


def as_row(components):
    return [(components[0], components[1]), (components[2], components[3])]


def flat(pairs):
    return jnp.concatenate([part for pair in pairs for part in pair], axis=1)


def tile_sums(share, samples, means, blocks, width):
    count = samples.shape[1] // width
    summed = dot(share, samples)
    n_tiles = share.shape[0] // (CLOG + 1)
    levels = []
    for i in range(count):
        part = summed[:, i * width : (i + 1) * width]
        levels.append(
            jnp.concatenate(
                [part[k * n_tiles : (k + 1) * n_tiles] for k in range(1, CLOG + 1)], axis=1
            )
        )
    spread = dot(jnp.concatenate(levels, axis=0).astype(BF16), means)
    result = []
    for i in range(count):
        part = summed[:n_tiles, i * width : (i + 1) * width]
        part = part + spread[i * n_tiles : (i + 1) * n_tiles]
        result.append(part.reshape(blocks, n_tiles // blocks, width))
    return jnp.concatenate(result, axis=1).astype(BF16)


def channel_average(samples, means, level, width):
    averaged = dot(samples, means)
    result = samples.astype(F32)
    for k in range(1, CLOG + 1):
        result = jnp.where(level >= k, averaged[:, (k - 1) * width : k * width], result)
    return result


def peers(mine, count):
    chips = count // 2
    chip = mine // 2
    core = lax.rem(mine, 2)
    others = []
    for step in range(1, chips):
        for flip in range(2):
            others.append(lax.rem(chip + step, chips) * 2 + lax.rem(core + flip, 2))
    return others + [chip * 2 + 1 - core]


def kernel(
    n_tm, n_chan,
    vis_hbm, gain_hbm, pairs_hbm, bands_hbm, map_hbm, order_hbm, avg_ref, early_tiles, late_tiles,
    vis_ref, gain_ref, pairs_ref, bands_ref, map_ref, order_ref, local, index,
    send, turned, gain_send, gains, table, chosen, partials, calibrated, early_send, late_send,
    turn_out, turn_in, gain_out, gain_in, tile_out, tile_in,
):
    me = lax.axis_index("tm")
    mine = lax.axis_index("chan")
    baselines = vis_ref.shape[1]
    width = vis_ref.shape[2]
    rows = baselines // n_tm
    stations = gain_ref.shape[1]
    padded = gain_send.shape[2]
    tile_rows = early_tiles.shape[1] // 2
    n_tiles = tile_rows * n_tm
    times = map_ref.shape[0]
    first_at, second_at, time_at, chan_at = range(times, times + 4)
    around = [lax.rem(me + step, n_tm) for step in range(1, n_tm)]
    across = peers(mine, n_chan)

    sources = (
        gain_hbm.at[0:4], order_hbm, gain_hbm.at[4:8], vis_hbm.at[0], pairs_hbm, bands_hbm, map_hbm
    )
    targets = (
        gain_ref.at[0:4], order_ref, gain_ref.at[4:8], vis_ref, pairs_ref, bands_ref, map_ref
    )
    loads = [
        pltpu.make_async_copy(source, target, local.at[i])
        for i, (source, target) in enumerate(zip(sources, targets))
    ]
    for load in loads:
        load.start()

    barrier = pltpu.get_barrier_semaphore()
    for other in around:
        pl.semaphore_signal(barrier, inc=1, device_id={"tm": other}, device_id_type=MESH)
    for other in across:
        pl.semaphore_signal(barrier, inc=1, device_id={"chan": other}, device_id_type=MESH)

    def pack_gains(half):
        for c in range(n_chan):
            block = jnp.concatenate(
                [
                    gain_ref[4 * half + i, :, c * width : (c + 1) * width] for i in range(4)
                ],
                axis=1,
            )
            if padded > stations:
                block = jnp.concatenate(
                    [block, jnp.zeros((padded - stations, 4 * width), F32)], axis=0
                )
            gain_send[half, c] = block.astype(BF16)

    def gain_copy(half, other, slot):
        return pltpu.make_async_remote_copy(
            src_ref=gain_send.at[half, other],
            dst_ref=gains.at[half, slot],
            send_sem=gain_out.at[half, other],
            recv_sem=gain_in.at[half, slot],
            device_id={"chan": other},
            device_id_type=MESH,
        )

    def turn_copy(other, slot):
        return pltpu.make_async_remote_copy(
            src_ref=send.at[other],
            dst_ref=turned.at[slot],
            send_sem=turn_out.at[other],
            recv_sem=turn_in.at[slot],
            device_id={"tm": other},
            device_id_type=MESH,
        )

    def tile_copy(chunk, other, slot):
        source, target = ((early_send, early_tiles), (late_send, late_tiles))[chunk]
        return pltpu.make_async_remote_copy(
            src_ref=source.at[other],
            dst_ref=target.at[slot],
            send_sem=tile_out.at[chunk, other],
            recv_sem=tile_in.at[chunk, slot],
            device_id={"tm": other},
            device_id_type=MESH,
        )

    copies = []

    def start(copy):
        copy.start()
        copies.append(copy)

    loads[0].wait()
    pack_gains(0)
    loads[1].wait()
    place = jnp.where(order_ref[...] == iota((baselines, baselines), 0), 1.0, 0.0)
    place = place.T.astype(BF16)

    pl.semaphore_wait(barrier, n_tm + n_chan - 2)

    for other in across:
        start(gain_copy(0, other, mine))
    loads[2].wait()
    pack_gains(1)
    for other in across:
        start(gain_copy(1, other, mine))

    loads[3].wait()
    raw = jnp.concatenate([vis_ref[i] for i in range(8)], axis=1)
    send[...] = dot(place, raw).astype(BF16).reshape(send.shape)
    for other in around:
        start(turn_copy(other, me))

    turned[me] = send[me]
    gains[0, mine] = gain_send[0, mine]
    gains[1, mine] = gain_send[1, mine]
    means = channel_means(width)
    stacked = jnp.concatenate(
        [means[:, k * width : (k + 1) * width] for k in range(CLOG)], axis=0
    )
    for load in loads[4:]:
        load.wait()
    index[...] = jnp.zeros_like(index)
    index[:times] = map_ref[...].astype(F32)
    index[first_at : second_at + 1] = pairs_ref[...].astype(F32)
    index[time_at : chan_at + 1] = bands_ref[...].astype(F32)
    table[...] = lax.dot_general(
        place, index[...].astype(BF16), (((1,), (1,)), ((), ())), preferred_element_type=F32
    )

    ids = iota((1, n_chan * padded), 1)
    if padded > stations:
        lane = ids
        for c in range(n_chan):
            inside = (lane >= c * padded) & (lane < c * padded + stations)
            ids = jnp.where(inside, lane - c * (padded - stations), ids)
            ids = jnp.where((lane >= c * padded + stations) & (lane < (c + 1) * padded), -1, ids)
    here = pl.ds(pl.multiple_of(me * rows, rows), rows)
    at_all = table[...].astype(jnp.int32)
    at_here = table[here, :].astype(jnp.int32)
    pick = jnp.concatenate(
        [
            one_hot(at_all[:, first_at : first_at + 1], ids),
            one_hot(at_all[:, second_at : second_at + 1], ids),
            one_hot(at_here[:, first_at : first_at + 1], ids),
            one_hot(at_here[:, second_at : second_at + 1], ids),
        ],
        axis=0,
    )
    period = jnp.left_shift(jnp.ones((baselines, 1), jnp.int32), at_all[:, time_at : time_at + 1])
    begin = me - (me & (period - 1))
    lane = iota((baselines, LANES), 1)
    tile = jnp.sum(
        jnp.where(lane == begin, table[...], 0.0), axis=1, keepdims=True
    ).astype(jnp.int32)
    tile = tile + n_tiles * at_all[:, chan_at : chan_at + 1]
    n_share = (CLOG + 1) * n_tiles
    wide = -(-n_share // LANES) * LANES
    share = jnp.where(tile == iota((baselines, wide), 1), 1.0 / period.astype(F32), 0.0)
    share = share.T[:n_share].astype(BF16)

    def block_rows(k):
        at = pl.ds(pl.multiple_of(k * rows, rows), rows)
        return at, pl.ds(pl.multiple_of(baselines + k * rows, rows), rows)

    for other in across:
        gain_copy(0, other, other).wait_recv()
    chosen[0] = dot(pick, gains[0].reshape(n_chan * padded, 4 * width))

    def calibrate_early(k, carry):
        at, at_second = block_rows(k)
        coherency = as_matrix(split(send[k].astype(F32), width))
        partial = row_times(as_row(split(chosen[0, at, :], width)), coherency)
        partials[at, :] = flat(partial)
        entry = times_row_conj(partial, as_row(split(chosen[0, at_second, :], width)))
        calibrated[at, : 2 * width] = flat([entry]).astype(BF16)
        return carry

    lax.fori_loop(0, n_tm, calibrate_early, 0, unroll=2)
    early_send[...] = tile_sums(share, calibrated[:, : 2 * width], stacked, n_tm, width)
    for other in around:
        start(tile_copy(0, other, me))
    early_tiles[me] = early_send[me]

    for other in across:
        gain_copy(1, other, other).wait_recv()
    chosen[1] = dot(pick, gains[1].reshape(n_chan * padded, 4 * width))

    def calibrate_late(k, carry):
        at, at_second = block_rows(k)
        coherency = as_matrix(split(send[k].astype(F32), width))
        upper = as_row(split(partials[at, :], width))
        lower = row_times(as_row(split(chosen[1, at, :], width)), coherency)
        right_upper = as_row(split(chosen[0, at_second, :], width))
        right_lower = as_row(split(chosen[1, at_second, :], width))
        entries = [
            times_row_conj(upper, right_lower),
            times_row_conj(lower, right_upper),
            times_row_conj(lower, right_lower),
        ]
        calibrated[at, 2 * width :] = flat(entries).astype(BF16)
        return carry

    lax.fori_loop(0, n_tm, calibrate_late, 0, unroll=2)
    late_send[...] = tile_sums(share, calibrated[:, 2 * width :], stacked, n_tm, width)
    for other in around:
        start(tile_copy(1, other, me))
    late_tiles[me] = late_send[me]

    for other in around:
        turn_copy(other, other).wait_recv()
    ends = (2 * baselines, 2 * baselines + rows, 2 * baselines + 2 * rows)
    left, right = [
        split(chosen[0, ends[j] : ends[j + 1], :], width)
        + split(chosen[1, ends[j] : ends[j + 1], :], width)
        for j in range(2)
    ]

    def calibrate_time(t, carry):
        result = jones_apply(left, split(turned[t].astype(F32), width), right)
        at = pl.ds(pl.multiple_of(t * rows, rows), rows)
        calibrated[at, :] = jnp.concatenate(result, axis=1).astype(BF16)
        return carry

    lax.fori_loop(0, n_tm, calibrate_time, 0, unroll=2)
    group = 2**TLOG
    time_level = jnp.broadcast_to(at_here[:, time_at : time_at + 1], (rows, width))
    chan_level = jnp.broadcast_to(at_here[:, chan_at : chan_at + 1], (rows, width))
    chan_level = jnp.concatenate([chan_level] * group, axis=0)
    for first in range(0, n_tm, group):
        at = slice(first * rows, (first + group) * rows)
        for i in range(8):
            part = channel_average(
                calibrated[at, i * width : (i + 1) * width], means, chan_level, width
            )
            current = [part[t * rows : (t + 1) * rows] for t in range(group)]
            result = list(current)
            for k in range(1, TLOG + 1):
                current = [
                    0.5 * (current[2 * j] + current[2 * j + 1]) for j in range(len(current) // 2)
                ]
                result = [
                    jnp.where(time_level >= k, current[t >> k], result[t]) for t in range(group)
                ]
            for t in range(group):
                avg_ref[first + t, i] = result[t].astype(BF16)

    for chunk in range(2):
        for other in around:
            tile_copy(chunk, other, other).wait_recv()
    for copy in copies:
        copy.wait_send()


def write_kernel(avg_ref, early_ref, late_ref, avg_hbm, grid_hbm, grid, done):
    averaged = pltpu.make_async_copy(avg_ref, avg_hbm, done.at[0])
    averaged.start()
    tile_rows = grid.shape[0]
    first = 0
    for ref in (early_ref, late_ref):
        total = ref[0].astype(F32)
        for m in range(1, ref.shape[0]):
            total = total + ref[m].astype(F32)
        count = ref.shape[1] // tile_rows
        for i in range(count):
            grid[:, first + i, :] = total[i * tile_rows : (i + 1) * tile_rows]
        first += count
    gridded = pltpu.make_async_copy(grid, grid_hbm, done.at[1])
    gridded.start()
    averaged.wait()
    gridded.wait()


def shards(n_tm, n_chan, tile_count, visibilities, station_gains, station_pairs, average_bands, tile_map, baseline_order):
    baselines, width = visibilities.shape[2:]
    rows = baselines // n_tm
    stations = station_gains.shape[1]
    padded = -(-stations // 16) * 16
    tile_rows = tile_count // n_tm
    vmem = pl.BlockSpec(memory_space=pltpu.VMEM)
    dma = pltpu.SemaphoreType.DMA
    hbm = functools.partial(pltpu.with_memory_space_constraint, memory_space=pltpu.HBM)
    near = functools.partial(pltpu.with_memory_space_constraint, memory_space=pltpu.VMEM)
    averaged, early, late = pl.pallas_call(
        functools.partial(kernel, n_tm, n_chan),
        out_shape=(
            pltpu.VMEM((n_tm, 8, rows, width), BF16),
            pltpu.VMEM((n_tm, 2 * tile_rows, width), BF16),
            pltpu.VMEM((n_tm, 6 * tile_rows, width), BF16),
        ),
        in_specs=[pl.BlockSpec(memory_space=pl.ANY)] * 6,
        out_specs=(vmem,) * 3,
        scratch_shapes=[
            pltpu.VMEM((8, baselines, width), BF16),
            pltpu.VMEM(station_gains.shape, F32),
            pltpu.VMEM((2, baselines), jnp.int32),
            pltpu.VMEM((2, baselines), jnp.int32),
            pltpu.VMEM((n_tm, baselines), jnp.int32),
            pltpu.VMEM((1, baselines), jnp.int32),
            dma((7,)),
            pltpu.VMEM((LANES, baselines), F32),
            pltpu.VMEM((n_tm, rows, 8 * width), BF16),
            pltpu.VMEM((n_tm, rows, 8 * width), BF16),
            pltpu.VMEM((2, n_chan, padded, 4 * width), BF16),
            pltpu.VMEM((2, n_chan, padded, 4 * width), BF16),
            pltpu.VMEM((baselines, LANES), F32),
            pltpu.VMEM((2, 2 * baselines + 2 * rows, 4 * width), F32),
            pltpu.VMEM((baselines, 4 * width), F32),
            pltpu.VMEM((baselines, 8 * width), BF16),
            pltpu.VMEM((n_tm, 2 * tile_rows, width), BF16),
            pltpu.VMEM((n_tm, 6 * tile_rows, width), BF16),
            dma((n_tm,)),
            dma((n_tm,)),
            dma((2, n_chan)),
            dma((2, n_chan)),
            dma((2, n_tm)),
            dma((2, n_tm)),
        ],
        compiler_params=pltpu.CompilerParams(
            collective_id=0, has_side_effects=True, vmem_limit_bytes=40 * 2**20
        ),
        cost_estimate=pl.CostEstimate(
            flops=2 * 10**8, bytes_accessed=2 * 10**6, transcendentals=0
        ),
    )(
        hbm(visibilities),
        hbm(station_gains),
        hbm(station_pairs.T),
        hbm(average_bands.T),
        hbm(tile_map.T),
        hbm(baseline_order.reshape(1, baselines)),
    )
    return pl.pallas_call(
        write_kernel,
        out_shape=(
            pltpu.HBM(averaged.shape, BF16),
            pltpu.HBM((tile_rows, 8, width), F32),
        ),
        in_specs=[vmem] * 3,
        out_specs=(pl.BlockSpec(memory_space=pltpu.HBM),) * 2,
        scratch_shapes=[pltpu.VMEM((tile_rows, 8, width), F32), dma((2,))],
        compiler_params=pltpu.CompilerParams(vmem_limit_bytes=8 * 2**20),
        cost_estimate=pl.CostEstimate(flops=10**6, bytes_accessed=10**6, transcendentals=0),
    )(near(averaged), near(early), near(late))


def solution(mesh):
    n_tm, n_chan = mesh.shape["tm"], mesh.shape["chan"]
    tile_count = 8 * n_tm
    return jax.shard_map(
        functools.partial(shards, n_tm, n_chan, tile_count),
        mesh=mesh,
        in_specs=(P("tm", None, None, "chan"), P(None, "chan", None), P(), P(), P(), P()),
        out_specs=(P(None, None, "tm", "chan"), P("tm", None, "chan")),
        check_vma=False,
    )
```

time: 18.4 us -> 18.1 us (0.984)
  Pallas kernels: 17.5 us -> 17.3 us
where the time goes in v5:
time: 18.1 us; the launch traced here: 18 us
  Pallas kernels  17.3 us (96%)
  between operations  0.64 us (4%)
    pallas_call x1, Pallas kernels, shards(): pl.pallas_call(functools.partial(kernel, n_tm, n_chan), out_shape=(pltpu....  16.6 us
    pallas_call x1, Pallas kernels, shards(): pl.pallas_call(write_kernel, out_shape=(pltpu.HBM(averaged.shape, BF16),...  0.72 us

profile of v5, /device:TPU:0, one launch (start us, length us, event | category | flops | bytes accessed | tf_op | source)
XLA Modules:
  0.0 18.0 jit_solution(6395866512912190445)
XLA Ops:
  0.6 16.6 %shard_map.77 = (bf16[8,8,16,128]{3,2,1,0:T(8,128)(2,1)S(1)}, bf16[8,16,128]{2,1,0:T(8,128)(2,1)S(1)}, bf16[8,48,128]{2,1,0:T(8,128)(2,1)S(1)}) custom-call(bf16[1,8,128,128]{3,2,1,0:T(8,128)(2,1)} %vis_hbm.1, f32[8,48,512]{2,1,0:T(8,128)} %gain_hbm.1, s32[2,128]{1,0:T(2,128)} %bitcast.5, s32[2,128]{1,0:T(2,128)} %bitcast.6, s32[8,128]{1,0:T(8,128)} %bitcast.4, ...), custom_call_target="tpu_custom_call" | custom-call | flops 200000000 | bytes 2000000 | tf_op jit(solution)/shard_map/pallas_call | solution.py:427
  17.3 0.7 %shard_map.78 = (bf16[8,8,16,128]{3,2,1,0:T(8,128)(2,1)}, f32[8,8,128]{2,1,0:T(8,128)}) custom-call(bf16[8,8,16,128]{3,2,1,0:T(8,128)(2,1)S(1)} %get-tuple-element.5.avg_ref, bf16[8,16,128]{2,1,0:T(8,128)(2,1)S(1)} %get-tuple-element.6.early_ref, bf16[8,48,128]{2,1,0:T(8,128)(2,1)S(1)} %get-tuple-element.7.late_ref), custom_call_target="tpu_custom_call" | custom-call | flops 1000000 | bytes 1000000 | tf_op jit(solution)/shard_map/pallas_call | solution.py:476

commit v6 on v5

--- a/solution.py
+++ b/solution.py
@@ -160,7 +160,7 @@
     n_tiles = tile_rows * n_tm
     times = map_ref.shape[0]
     first_at, second_at, time_at, chan_at = range(times, times + 4)
-    around = [lax.rem(me + step, n_tm) for step in range(1, n_tm)]
+    around = [step + lax.div(step - me + n_tm, n_tm) for step in range(n_tm - 1)]
     across = peers(mine, n_chan)
 
     sources = (

time: 18.1 us -> 18.1 us (level)
  no operation moved by 1% of the time
where the time goes in v6:
time: 18.1 us; the launch traced here: 18 us
  Pallas kernels  17.3 us (96%)
  between operations  0.64 us (4%)
    pallas_call x1, Pallas kernels, shards(): pl.pallas_call(functools.partial(kernel, n_tm, n_chan), out_shape=(pltpu....  16.6 us
    pallas_call x1, Pallas kernels, shards(): pl.pallas_call(write_kernel, out_shape=(pltpu.HBM(averaged.shape, BF16),...  0.72 us

profile of v6, /device:TPU:0, one launch (start us, length us, event | category | flops | bytes accessed | tf_op | source)
XLA Modules:
  0.0 18.0 jit_solution(6085721720084077096)
XLA Ops:
  0.6 16.6 %shard_map.77 = (bf16[8,8,16,128]{3,2,1,0:T(8,128)(2,1)S(1)}, bf16[8,16,128]{2,1,0:T(8,128)(2,1)S(1)}, bf16[8,48,128]{2,1,0:T(8,128)(2,1)S(1)}) custom-call(bf16[1,8,128,128]{3,2,1,0:T(8,128)(2,1)} %vis_hbm.1, f32[8,48,512]{2,1,0:T(8,128)} %gain_hbm.1, s32[2,128]{1,0:T(2,128)} %bitcast.5, s32[2,128]{1,0:T(2,128)} %bitcast.6, s32[8,128]{1,0:T(8,128)} %bitcast.4, ...), custom_call_target="tpu_custom_call" | custom-call | flops 200000000 | bytes 2000000 | tf_op jit(solution)/shard_map/pallas_call | solution.py:427
  17.2 0.7 %shard_map.78 = (bf16[8,8,16,128]{3,2,1,0:T(8,128)(2,1)}, f32[8,8,128]{2,1,0:T(8,128)}) custom-call(bf16[8,8,16,128]{3,2,1,0:T(8,128)(2,1)S(1)} %get-tuple-element.5.avg_ref, bf16[8,16,128]{2,1,0:T(8,128)(2,1)S(1)} %get-tuple-element.6.early_ref, bf16[8,48,128]{2,1,0:T(8,128)(2,1)S(1)} %get-tuple-element.7.late_ref), custom_call_target="tpu_custom_call" | custom-call | flops 1000000 | bytes 1000000 | tf_op jit(solution)/shard_map/pallas_call | solution.py:476

commit v7 on v6

--- a/solution.py
+++ b/solution.py
@@ -9,6 +9,7 @@
 
 TLOG = 3
 CLOG = 2
+TILE_BITS = 3
 LANES = 128
 MESH = pl.DeviceIdType.MESH
 F32 = jnp.float32
@@ -146,8 +147,9 @@
     n_tm, n_chan,
     vis_hbm, gain_hbm, pairs_hbm, bands_hbm, map_hbm, order_hbm, avg_ref, early_tiles, late_tiles,
     vis_ref, gain_ref, pairs_ref, bands_ref, map_ref, order_ref, local, index,
-    send, turned, gain_send, gains, table, chosen, partials, calibrated, early_send, late_send,
-    turn_out, turn_in, gain_out, gain_in, tile_out, tile_in,
+    send, turned, gain_send, gains, table, chosen, partials, calibrated,
+    early_send, late_send, early_pair, late_pair, early_sum, late_sum,
+    turn_out, turn_in, gain_out, gain_in, tile_out, tile_in, pair_out, pair_in,
 ):
     me = lax.axis_index("tm")
     mine = lax.axis_index("chan")
@@ -162,6 +164,10 @@
     first_at, second_at, time_at, chan_at = range(times, times + 4)
     around = [step + lax.div(step - me + n_tm, n_tm) for step in range(n_tm - 1)]
     across = peers(mine, n_chan)
+    half = n_tm // 2
+    line = lax.rem(me, 2)
+    spot = lax.div(me, 2)
+    spots = [lax.rem(spot + step, half) for step in range(1, half)]
 
     sources = (
         gain_hbm.at[0:4], order_hbm, gain_hbm.at[4:8], vis_hbm.at[0], pairs_hbm, bands_hbm, map_hbm
@@ -216,16 +222,41 @@
             device_id_type=MESH,
         )
 
+    chunks = (
+        (early_send, early_pair, early_sum, early_tiles),
+        (late_send, late_pair, late_sum, late_tiles),
+    )
+
+    def pair_copy(chunk):
+        source, target = chunks[chunk][:2]
+        return pltpu.make_async_remote_copy(
+            src_ref=source.at[pl.ds((1 - line) * half, half)],
+            dst_ref=target,
+            send_sem=pair_out.at[chunk],
+            recv_sem=pair_in.at[chunk],
+            device_id={"tm": spot * 2 + 1 - line},
+            device_id_type=MESH,
+        )
+
     def tile_copy(chunk, other, slot):
-        source, target = ((early_send, early_tiles), (late_send, late_tiles))[chunk]
+        source, target = chunks[chunk][2:]
         return pltpu.make_async_remote_copy(
             src_ref=source.at[other],
             dst_ref=target.at[slot],
             send_sem=tile_out.at[chunk, other],
             recv_sem=tile_in.at[chunk, slot],
-            device_id={"tm": other},
+            device_id={"tm": other * 2 + line},
             device_id_type=MESH,
         )
+
+    def pass_on(chunk):
+        own, pair, both, target = chunks[chunk]
+        pair_copy(chunk).wait_recv()
+        total = own[pl.ds(line * half, half)].astype(F32) + pair[...].astype(F32)
+        both[...] = total.astype(BF16)
+        for other in spots:
+            start(tile_copy(chunk, other, spot))
+        target[spot] = both[spot]
 
     copies = []
 
@@ -296,6 +327,8 @@
     tile = jnp.sum(
         jnp.where(lane == begin, table[...], 0.0), axis=1, keepdims=True
     ).astype(jnp.int32)
+    owner = tile >> TILE_BITS
+    tile = (((owner & 1) * half + (owner >> 1)) << TILE_BITS) + (tile & (tile_rows - 1))
     tile = tile + n_tiles * at_all[:, chan_at : chan_at + 1]
     n_share = (CLOG + 1) * n_tiles
     wide = -(-n_share // LANES) * LANES
@@ -321,9 +354,7 @@
 
     lax.fori_loop(0, n_tm, calibrate_early, 0, unroll=2)
     early_send[...] = tile_sums(share, calibrated[:, : 2 * width], stacked, n_tm, width)
-    for other in around:
-        start(tile_copy(0, other, me))
-    early_tiles[me] = early_send[me]
+    start(pair_copy(0))
 
     for other in across:
         gain_copy(1, other, other).wait_recv()
@@ -345,10 +376,10 @@
         return carry
 
     lax.fori_loop(0, n_tm, calibrate_late, 0, unroll=2)
+    pass_on(0)
     late_send[...] = tile_sums(share, calibrated[:, 2 * width :], stacked, n_tm, width)
-    for other in around:
-        start(tile_copy(1, other, me))
-    late_tiles[me] = late_send[me]
+    start(pair_copy(1))
+    pass_on(1)
 
     for other in around:
         turn_copy(other, other).wait_recv()
@@ -389,7 +420,7 @@
                 avg_ref[first + t, i] = result[t].astype(BF16)
 
     for chunk in range(2):
-        for other in around:
+        for other in spots:
             tile_copy(chunk, other, other).wait_recv()
     for copy in copies:
         copy.wait_send()
@@ -428,8 +459,8 @@
         functools.partial(kernel, n_tm, n_chan),
         out_shape=(
             pltpu.VMEM((n_tm, 8, rows, width), BF16),
-            pltpu.VMEM((n_tm, 2 * tile_rows, width), BF16),
-            pltpu.VMEM((n_tm, 6 * tile_rows, width), BF16),
+            pltpu.VMEM((n_tm // 2, 2 * tile_rows, width), BF16),
+            pltpu.VMEM((n_tm // 2, 6 * tile_rows, width), BF16),
         ),
         in_specs=[pl.BlockSpec(memory_space=pl.ANY)] * 6,
         out_specs=(vmem,) * 3,
@@ -452,12 +483,18 @@
             pltpu.VMEM((baselines, 8 * width), BF16),
             pltpu.VMEM((n_tm, 2 * tile_rows, width), BF16),
             pltpu.VMEM((n_tm, 6 * tile_rows, width), BF16),
+            pltpu.VMEM((n_tm // 2, 2 * tile_rows, width), BF16),
+            pltpu.VMEM((n_tm // 2, 6 * tile_rows, width), BF16),
+            pltpu.VMEM((n_tm // 2, 2 * tile_rows, width), BF16),
+            pltpu.VMEM((n_tm // 2, 6 * tile_rows, width), BF16),
             dma((n_tm,)),
             dma((n_tm,)),
             dma((2, n_chan)),
             dma((2, n_chan)),
-            dma((2, n_tm)),
-            dma((2, n_tm)),
+            dma((2, n_tm // 2)),
+            dma((2, n_tm // 2)),
+            dma((2,)),
+            dma((2,)),
         ],
         compiler_params=pltpu.CompilerParams(
             collective_id=0, has_side_effects=True, vmem_limit_bytes=40 * 2**20
@@ -489,7 +526,7 @@
 
 def solution(mesh):
     n_tm, n_chan = mesh.shape["tm"], mesh.shape["chan"]
-    tile_count = 8 * n_tm
+    tile_count = n_tm << TILE_BITS
     return jax.shard_map(
         functools.partial(shards, n_tm, n_chan, tile_count),
         mesh=mesh,

time: 18.1 us -> 21.7 us (1.20)
  Pallas kernels: 17.3 us -> 20.9 us
    pallas_call x1, Pallas kernels: 16.6 us -> 20.2 us  [shards(): pl.pallas_call(functools.partial(kernel, n_tm, n_chan), out_shape=(pltpu....]
where the time goes in v7:
time: 21.7 us; the launch traced here: 21.5 us
  Pallas kernels  20.9 us (96%)
  between operations  0.64 us (3%)
    pallas_call x1, Pallas kernels, shards(): pl.pallas_call(functools.partial(kernel, n_tm, n_chan), out_shape=(pltpu....  20.2 us
    pallas_call x1, Pallas kernels, shards(): pl.pallas_call(write_kernel, out_shape=(pltpu.HBM(averaged.shape, BF16),...  0.72 us

profile of v7, /device:TPU:0, one launch (start us, length us, event | category | flops | bytes accessed | tf_op | source)
XLA Modules:
  0.0 21.5 jit_solution(4647565428665756327)
XLA Ops:
  0.6 20.2 %shard_map.77 = (bf16[8,8,16,128]{3,2,1,0:T(8,128)(2,1)S(1)}, bf16[4,16,128]{2,1,0:T(8,128)(2,1)S(1)}, bf16[4,48,128]{2,1,0:T(8,128)(2,1)S(1)}) custom-call(bf16[1,8,128,128]{3,2,1,0:T(8,128)(2,1)} %vis_hbm.1, f32[8,48,512]{2,1,0:T(8,128)} %gain_hbm.1, s32[2,128]{1,0:T(2,128)} %bitcast.5, s32[2,128]{1,0:T(2,128)} %bitcast.6, s32[8,128]{1,0:T(8,128)} %bitcast.4, ...), custom_call_target="tpu_custom_call" | custom-call | flops 200000000 | bytes 2000000 | tf_op jit(solution)/shard_map/pallas_call | solution.py:458
  20.8 0.7 %shard_map.78 = (bf16[8,8,16,128]{3,2,1,0:T(8,128)(2,1)}, f32[8,8,128]{2,1,0:T(8,128)}) custom-call(bf16[8,8,16,128]{3,2,1,0:T(8,128)(2,1)S(1)} %get-tuple-element.5.avg_ref, bf16[4,16,128]{2,1,0:T(8,128)(2,1)S(1)} %get-tuple-element.6.early_ref, bf16[4,48,128]{2,1,0:T(8,128)(2,1)S(1)} %get-tuple-element.7.late_ref), custom_call_target="tpu_custom_call" | custom-call | flops 1000000 | bytes 1000000 | tf_op jit(solution)/shard_map/pallas_call | solution.py:513

commit v8 on v6

--- a/solution.py
+++ b/solution.py
@@ -239,20 +239,20 @@
     place = jnp.where(order_ref[...] == iota((baselines, baselines), 0), 1.0, 0.0)
     place = place.T.astype(BF16)
 
-    pl.semaphore_wait(barrier, n_tm + n_chan - 2)
-
-    for other in across:
-        start(gain_copy(0, other, mine))
-    loads[2].wait()
-    pack_gains(1)
-    for other in across:
-        start(gain_copy(1, other, mine))
-
     loads[3].wait()
     raw = jnp.concatenate([vis_ref[i] for i in range(8)], axis=1)
     send[...] = dot(place, raw).astype(BF16).reshape(send.shape)
+    loads[2].wait()
+    pack_gains(1)
+
+    pl.semaphore_wait(barrier, n_tm + n_chan - 2)
+
+    for other in across:
+        start(gain_copy(0, other, mine))
     for other in around:
         start(turn_copy(other, me))
+    for other in across:
+        start(gain_copy(1, other, mine))
 
     turned[me] = send[me]
     gains[0, mine] = gain_send[0, mine]

time: 18.1 us -> 18.2 us (level)
  no operation moved by 1% of the time
where the time goes in v8:
time: 18.2 us; the launch traced here: 18.1 us
  Pallas kernels  17.4 us (96%)
  between operations  0.64 us (4%)
    pallas_call x1, Pallas kernels, shards(): pl.pallas_call(functools.partial(kernel, n_tm, n_chan), out_shape=(pltpu....  16.7 us
    pallas_call x1, Pallas kernels, shards(): pl.pallas_call(write_kernel, out_shape=(pltpu.HBM(averaged.shape, BF16),...  0.72 us

profile of v8, /device:TPU:0, one launch (start us, length us, event | category | flops | bytes accessed | tf_op | source)
XLA Modules:
  0.0 18.1 jit_solution(3611877947049568082)
XLA Ops:
  0.6 16.7 %shard_map.77 = (bf16[8,8,16,128]{3,2,1,0:T(8,128)(2,1)S(1)}, bf16[8,16,128]{2,1,0:T(8,128)(2,1)S(1)}, bf16[8,48,128]{2,1,0:T(8,128)(2,1)S(1)}) custom-call(bf16[1,8,128,128]{3,2,1,0:T(8,128)(2,1)} %vis_hbm.1, f32[8,48,512]{2,1,0:T(8,128)} %gain_hbm.1, s32[2,128]{1,0:T(2,128)} %bitcast.5, s32[2,128]{1,0:T(2,128)} %bitcast.6, s32[8,128]{1,0:T(8,128)} %bitcast.4, ...), custom_call_target="tpu_custom_call" | custom-call | flops 200000000 | bytes 2000000 | tf_op jit(solution)/shard_map/pallas_call | solution.py:427
  17.3 0.7 %shard_map.78 = (bf16[8,8,16,128]{3,2,1,0:T(8,128)(2,1)}, f32[8,8,128]{2,1,0:T(8,128)}) custom-call(bf16[8,8,16,128]{3,2,1,0:T(8,128)(2,1)S(1)} %get-tuple-element.5.avg_ref, bf16[8,16,128]{2,1,0:T(8,128)(2,1)S(1)} %get-tuple-element.6.early_ref, bf16[8,48,128]{2,1,0:T(8,128)(2,1)S(1)} %get-tuple-element.7.late_ref), custom_call_target="tpu_custom_call" | custom-call | flops 1000000 | bytes 1000000 | tf_op jit(solution)/shard_map/pallas_call | solution.py:476

commit v9 on v6

--- a/solution.py
+++ b/solution.py
@@ -319,7 +319,7 @@
         calibrated[at, : 2 * width] = flat([entry]).astype(BF16)
         return carry
 
-    lax.fori_loop(0, n_tm, calibrate_early, 0, unroll=2)
+    lax.fori_loop(0, n_tm, calibrate_early, 0, unroll=4)
     early_send[...] = tile_sums(share, calibrated[:, : 2 * width], stacked, n_tm, width)
     for other in around:
         start(tile_copy(0, other, me))
@@ -344,7 +344,7 @@
         calibrated[at, 2 * width :] = flat(entries).astype(BF16)
         return carry
 
-    lax.fori_loop(0, n_tm, calibrate_late, 0, unroll=2)
+    lax.fori_loop(0, n_tm, calibrate_late, 0, unroll=4)
     late_send[...] = tile_sums(share, calibrated[:, 2 * width :], stacked, n_tm, width)
     for other in around:
         start(tile_copy(1, other, me))
@@ -365,7 +365,7 @@
         calibrated[at, :] = jnp.concatenate(result, axis=1).astype(BF16)
         return carry
 
-    lax.fori_loop(0, n_tm, calibrate_time, 0, unroll=2)
+    lax.fori_loop(0, n_tm, calibrate_time, 0, unroll=4)
     group = 2**TLOG
     time_level = jnp.broadcast_to(at_here[:, time_at : time_at + 1], (rows, width))
     chan_level = jnp.broadcast_to(at_here[:, chan_at : chan_at + 1], (rows, width))

time: 18.1 us -> 18.1 us (level)
  no operation moved by 1% of the time
where the time goes in v9:
time: 18.1 us; the launch traced here: 17.9 us
  Pallas kernels  17.3 us (96%)
  between operations  0.64 us (4%)
    pallas_call x1, Pallas kernels, shards(): pl.pallas_call(functools.partial(kernel, n_tm, n_chan), out_shape=(pltpu....  16.6 us
    pallas_call x1, Pallas kernels, shards(): pl.pallas_call(write_kernel, out_shape=(pltpu.HBM(averaged.shape, BF16),...  0.72 us

profile of v9, /device:TPU:0, one launch (start us, length us, event | category | flops | bytes accessed | tf_op | source)
XLA Modules:
  0.0 17.9 jit_solution(16833467607275122394)
XLA Ops:
  0.6 16.6 %shard_map.77 = (bf16[8,8,16,128]{3,2,1,0:T(8,128)(2,1)S(1)}, bf16[8,16,128]{2,1,0:T(8,128)(2,1)S(1)}, bf16[8,48,128]{2,1,0:T(8,128)(2,1)S(1)}) custom-call(bf16[1,8,128,128]{3,2,1,0:T(8,128)(2,1)} %vis_hbm.1, f32[8,48,512]{2,1,0:T(8,128)} %gain_hbm.1, s32[2,128]{1,0:T(2,128)} %bitcast.5, s32[2,128]{1,0:T(2,128)} %bitcast.6, s32[8,128]{1,0:T(8,128)} %bitcast.4, ...), custom_call_target="tpu_custom_call" | custom-call | flops 200000000 | bytes 2000000 | tf_op jit(solution)/shard_map/pallas_call | solution.py:427
  17.2 0.7 %shard_map.78 = (bf16[8,8,16,128]{3,2,1,0:T(8,128)(2,1)}, f32[8,8,128]{2,1,0:T(8,128)}) custom-call(bf16[8,8,16,128]{3,2,1,0:T(8,128)(2,1)S(1)} %get-tuple-element.5.avg_ref, bf16[8,16,128]{2,1,0:T(8,128)(2,1)S(1)} %get-tuple-element.6.early_ref, bf16[8,48,128]{2,1,0:T(8,128)(2,1)S(1)} %get-tuple-element.7.late_ref), custom_call_target="tpu_custom_call" | custom-call | flops 1000000 | bytes 1000000 | tf_op jit(solution)/shard_map/pallas_call | solution.py:476

commit v10 on v8

--- a/solution.py
+++ b/solution.py
@@ -239,24 +239,6 @@
     place = jnp.where(order_ref[...] == iota((baselines, baselines), 0), 1.0, 0.0)
     place = place.T.astype(BF16)
 
-    loads[3].wait()
-    raw = jnp.concatenate([vis_ref[i] for i in range(8)], axis=1)
-    send[...] = dot(place, raw).astype(BF16).reshape(send.shape)
-    loads[2].wait()
-    pack_gains(1)
-
-    pl.semaphore_wait(barrier, n_tm + n_chan - 2)
-
-    for other in across:
-        start(gain_copy(0, other, mine))
-    for other in around:
-        start(turn_copy(other, me))
-    for other in across:
-        start(gain_copy(1, other, mine))
-
-    turned[me] = send[me]
-    gains[0, mine] = gain_send[0, mine]
-    gains[1, mine] = gain_send[1, mine]
     means = channel_means(width)
     stacked = jnp.concatenate(
         [means[:, k * width : (k + 1) * width] for k in range(CLOG)], axis=0
@@ -302,6 +284,24 @@
     share = jnp.where(tile == iota((baselines, wide), 1), 1.0 / period.astype(F32), 0.0)
     share = share.T[:n_share].astype(BF16)
 
+    pl.semaphore_wait(barrier, n_tm + n_chan - 2)
+
+    for other in across:
+        start(gain_copy(0, other, mine))
+    loads[2].wait()
+    pack_gains(1)
+    for other in across:
+        start(gain_copy(1, other, mine))
+
+    loads[3].wait()
+    raw = jnp.concatenate([vis_ref[i] for i in range(8)], axis=1)
+    send[...] = dot(place, raw).astype(BF16).reshape(send.shape)
+    for other in around:
+        start(turn_copy(other, me))
+
+    turned[me] = send[me]
+    gains[0, mine] = gain_send[0, mine]
+    gains[1, mine] = gain_send[1, mine]
     def block_rows(k):
         at = pl.ds(pl.multiple_of(k * rows, rows), rows)
         return at, pl.ds(pl.multiple_of(baselines + k * rows, rows), rows)

time: 18.2 us -> 18.4 us (1.011)
  Pallas kernels: 17.4 us -> 17.6 us
    pallas_call x1, Pallas kernels: 16.7 us -> 16.9 us  [shards(): pl.pallas_call(functools.partial(kernel, n_tm, n_chan), out_shape=(pltpu....]
where the time goes in v10:
time: 18.4 us; the launch traced here: 18.3 us
  Pallas kernels  17.6 us (96%)
  between operations  0.64 us (3%)
    pallas_call x1, Pallas kernels, shards(): pl.pallas_call(functools.partial(kernel, n_tm, n_chan), out_shape=(pltpu....  16.9 us
    pallas_call x1, Pallas kernels, shards(): pl.pallas_call(write_kernel, out_shape=(pltpu.HBM(averaged.shape, BF16),...  0.72 us

profile of v10, /device:TPU:0, one launch (start us, length us, event | category | flops | bytes accessed | tf_op | source)
XLA Modules:
  0.0 18.3 jit_solution(18363780590274160005)
XLA Ops:
  0.6 16.9 %shard_map.77 = (bf16[8,8,16,128]{3,2,1,0:T(8,128)(2,1)S(1)}, bf16[8,16,128]{2,1,0:T(8,128)(2,1)S(1)}, bf16[8,48,128]{2,1,0:T(8,128)(2,1)S(1)}) custom-call(bf16[1,8,128,128]{3,2,1,0:T(8,128)(2,1)} %vis_hbm.1, f32[8,48,512]{2,1,0:T(8,128)} %gain_hbm.1, s32[2,128]{1,0:T(2,128)} %bitcast.5, s32[2,128]{1,0:T(2,128)} %bitcast.6, s32[8,128]{1,0:T(8,128)} %bitcast.4, ...), custom_call_target="tpu_custom_call" | custom-call | flops 200000000 | bytes 2000000 | tf_op jit(solution)/shard_map/pallas_call | solution.py:427
  17.5 0.7 %shard_map.78 = (bf16[8,8,16,128]{3,2,1,0:T(8,128)(2,1)}, f32[8,8,128]{2,1,0:T(8,128)}) custom-call(bf16[8,8,16,128]{3,2,1,0:T(8,128)(2,1)S(1)} %get-tuple-element.5.avg_ref, bf16[8,16,128]{2,1,0:T(8,128)(2,1)S(1)} %get-tuple-element.6.early_ref, bf16[8,48,128]{2,1,0:T(8,128)(2,1)S(1)} %get-tuple-element.7.late_ref), custom_call_target="tpu_custom_call" | custom-call | flops 1000000 | bytes 1000000 | tf_op jit(solution)/shard_map/pallas_call | solution.py:476
